TPU v7x, 32 devices: a whole 2x2x4 slice. The times are simulated.
32 devices in a mesh: frame: 16 (over z, y, x), space: 2 (over core).
Axes of the slice: x: 2, y: 2, z: 4, core: 2. Of those that a mesh axis runs over, the one named last changes fastest.
Arguments:
- block_input: bfloat16 [2, 4096, 768], P(None, ('frame', 'space')), may hold values from -6 to 6
- norm1_gain: float32 [768], replicated, may hold values from 0.5 to 1.5
- w_query: bfloat16 [768, 768], replicated, may hold values from -0.3125 to 0.3125
- w_key: bfloat16 [768, 768], replicated, may hold values from -0.3125 to 0.3125
- w_value: bfloat16 [768, 768], replicated, may hold values from -0.21875 to 0.21875
- w_out: bfloat16 [768, 768], replicated, may hold values from -1.75 to 1.75
- norm2_gain: float32 [768], replicated, may hold values from 0.5 to 1.5
- w_up: bfloat16 [768, 3072], replicated, may hold values from -0.21875 to 0.21875
- w_down: bfloat16 [3072, 768], replicated, may hold values from -0.109375 to 0.109375
- clip_frames: int32 [2, 4], replicated, may hold values from 0 to 16, as said below
- cotangent: bfloat16 [2, 4096, 768], P(None, ('frame', 'space')), may hold values from -6 to 6
Outputs:
- block_output: bfloat16 [2, 4096, 768], P(None, ('frame', 'space'))
- grad_input: float32 [2, 4096, 768], P(None, ('frame', 'space'))
- grad_norm1_gain: float32 [768], replicated
- grad_w_query: float32 [768, 768], replicated
- grad_w_key: float32 [768, 768], replicated
- grad_w_value: float32 [768, 768], replicated
- grad_w_out: float32 [768, 768], replicated
- grad_norm2_gain: float32 [768], replicated
- grad_w_up: float32 [768, 3072], replicated
- grad_w_down: float32 [3072, 768], replicated
Inputs may be any that keep to these rules, and one draw needn't show every extreme that they name: `clip_frames`: row s lists the lengths in frames of stream s's clips in order; each row sums to 16; a length is 0 or a multiple of 4, and zeros come only after the last clip; in one stream, drawn from the seed, a single clip holds all 16 frames.
All inputs are finite; a program needn't handle non-finite values.
Results may differ from a plain program's by a relative error of at most 0.017.
Values may be sent and summed in bfloat16 or wider, within the bound.
No kernel may reach another device: no remote copies, remote signals or barrier semaphores. Data moves between devices by JAX's collectives and lax.ppermute only.
A program may use at most 320 MiB of HBM per device.

v0:
```python
import math

import jax
import jax.numpy as jnp
from jax import lax
from jax.sharding import PartitionSpec as P

HEADS = 12
HEAD_DIM = 64


def layer_norm(values, gain_vector):
    average = jnp.mean(values, axis=-1, keepdims=True)
    centred = values - average
    spread = jnp.mean(centred * centred, axis=-1, keepdims=True)
    return centred * lax.rsqrt(spread + 1e-05) * gain_vector


def frame_tables(clip_frames, clip_first, frame_count):
    clip_ends = jnp.cumsum(clip_frames, axis=1, dtype=jnp.int32)
    clip_begins = clip_ends - clip_frames
    frame_index = jnp.arange(frame_count, dtype=jnp.int32)
    inside = (frame_index[None, :, None] >= clip_begins[:, None, :]) & (
        frame_index[None, :, None] < clip_ends[:, None, :]
    )
    frame_begin = jnp.sum(jnp.where(inside, clip_begins[:, None, :], 0), axis=2, dtype=jnp.int32)
    offsets = jnp.sum(
        jnp.where(inside, clip_first[:, None, :] - clip_begins[:, None, :], 0),
        axis=2,
        dtype=jnp.int32,
    )
    return (frame_begin, offsets + frame_index[None, :])


def lookup(table, frames):
    frame_count = table.shape[1]
    matches = jnp.arange(frame_count, dtype=jnp.int32)[None, None, :] == frames[:, :, None]
    return jnp.sum(jnp.where(matches, table[:, None, :], 0), axis=2, dtype=jnp.int32)


def rotate(values, cosine, sine_table):
    half_width = values.shape[-1] // 2
    turned = jnp.concatenate([-values[..., half_width:], values[..., :half_width]], axis=-1)
    return values * cosine + turned * sine_table


def flat_dot(left, right):
    return jnp.dot(left, right, preferred_element_type=jnp.float32)


def outer_dot(left, right):
    return lax.dot_general(
        left, right, (((0,), (0,)), ((), ())), preferred_element_type=jnp.float32
    )


def back_dot(left, right):
    return lax.dot_general(
        left, right, (((1,), (1,)), ((), ())), preferred_element_type=jnp.float32
    )


def over_blocks(carry, pieces, work):
    length = pieces[0].shape[1]
    step_rows = min(512, length)
    block_count = length // step_rows

    def one_block(block_index, state):
        first_row = block_index * step_rows
        block = tuple(
            (lax.dynamic_slice_in_dim(member, first_row, step_rows, 1) for member in pieces)
        )
        return work(state, block, first_row)

    carry = lax.fori_loop(0, block_count, one_block, carry)
    return carry


def local(
    block_input,
    norm1_gain,
    w_query,
    w_key,
    w_value,
    w_out,
    norm2_gain,
    w_up,
    w_down,
    clip_frames,
    cotangent,
):
    streams, local_rows, width = block_input.shape
    heads = HEADS
    head_width = HEAD_DIM
    scale_factor = 1.0 / math.sqrt(head_width)
    frame_count = lax.axis_size("frame")
    space_count = lax.axis_size("space")
    per_frame = local_rows * space_count
    flip_rows = jnp.arange(streams, dtype=jnp.int32) % 2 == 1
    flip_rows = jnp.zeros((streams,), dtype=jnp.bool_)
    frame_place = lax.axis_index("frame")
    space_place = lax.axis_index("space")

    def frame_of(device):
        return jnp.where(flip_rows[:, None], device[None, :], device[None, :])

    my_frame = frame_of(jnp.reshape(frame_place, (1,)))[:, 0]
    frame_begin, frame_time = frame_tables(clip_frames, jnp.zeros_like(clip_frames), frame_count)
    my_begin = lookup(frame_begin, my_frame[:, None])[:, 0]
    my_time = lookup(frame_time, my_frame[:, None])[:, 0]
    within = space_place * local_rows + jnp.arange(local_rows, dtype=jnp.int32)
    position = my_time[:, None] * per_frame + within[None, :]
    half_width = head_width // 2
    frequency = jnp.exp(
        jnp.arange(half_width, dtype=jnp.float32) * (-2.0 * math.log(10000.0) / head_width)
    )
    angles = position.astype(jnp.float32)[:, :, None] * frequency[None, None, :]
    cosine = jnp.concatenate([jnp.cos(angles), jnp.cos(angles)], axis=-1)[:, :, None, :]
    sine_table = jnp.concatenate([jnp.sin(angles), jnp.sin(angles)], axis=-1)[:, :, None, :]

    def rope_flat(values):
        return rotate(
            values.reshape(streams, local_rows, heads, head_width), cosine, sine_table
        ).reshape(streams, local_rows, width)

    tokens = streams * local_rows
    input_flat = block_input.astype(jnp.float32).reshape(tokens, width)
    normed = layer_norm(input_flat, norm1_gain).astype(jnp.bfloat16)
    query = rope_flat(flat_dot(normed, w_query)).astype(jnp.bfloat16)
    key_rows = rope_flat(flat_dot(normed, w_key)).astype(jnp.bfloat16)
    value_rows = flat_dot(normed, w_value).astype(jnp.bfloat16).reshape(streams, local_rows, width)
    query_four = query.reshape(streams, local_rows, heads, head_width)

    def key_mask(first_row, length):
        device = (first_row + jnp.arange(length, dtype=jnp.int32)) // per_frame
        frames = frame_of(device)
        return (frames >= my_begin[:, None]) & (frames <= my_frame[:, None])

    def attend(state, block, first_row):
        key_block, value_block = block
        length = key_block.shape[1]
        allowed = key_mask(first_row, length)

        def attend_compute(previous):
            top_old, total_old, summed_old = previous
            key_four = key_block.reshape(streams, length, heads, head_width)
            value_four = value_block.reshape(streams, length, heads, head_width)
            scores = (
                jnp.einsum(
                    "bqhd,bkhd->bhqk", query_four, key_four, preferred_element_type=jnp.float32
                )
                * scale_factor
            )
            keeper = allowed[:, None, None, :]
            top_new = jnp.maximum(top_old, jnp.max(jnp.where(keeper, scores, -1e30), axis=-1))
            weights = jnp.where(keeper, jnp.exp(scores - top_new[..., None]), 0.0)
            factor = jnp.exp(top_old - top_new)
            total_new = total_old * factor + jnp.sum(weights, axis=-1)
            summed_new = summed_old * factor[..., None] + jnp.einsum(
                "bhqk,bkhd->bhqd",
                weights.astype(jnp.bfloat16),
                value_four,
                preferred_element_type=jnp.float32,
            )
            return (top_new, total_new, summed_new)

        return lax.cond(jnp.any(allowed), attend_compute, lambda previous: previous, state)

    start_state = (
        jnp.full((streams, heads, local_rows), -1e30, jnp.float32),
        jnp.zeros((streams, heads, local_rows), jnp.float32),
        jnp.zeros((streams, heads, local_rows, head_width), jnp.float32),
    )
    keys_whole, values_whole = (
        lax.all_gather(key_rows, "space", axis=1, tiled=True),
        lax.all_gather(value_rows, "space", axis=1, tiled=True),
    )
    top_final, total_final, summed_final = over_blocks(
        start_state,
        (
            lax.all_gather(keys_whole, "frame", axis=1, tiled=True),
            lax.all_gather(values_whole, "frame", axis=1, tiled=True),
        ),
        attend,
    )
    attended = summed_final / total_final[..., None]
    log_total = top_final + jnp.log(total_final)
    attended_flat = attended.transpose(0, 2, 1, 3).reshape(tokens, width)
    attended_low = attended_flat.astype(jnp.bfloat16)
    middle = input_flat + flat_dot(attended_low, w_out)
    normed_two = layer_norm(middle, norm2_gain).astype(jnp.bfloat16)
    hidden = flat_dot(normed_two, w_up)
    activated, gelu_back = jax.vjp(lambda inner: jax.nn.gelu(inner, approximate=True), hidden)
    activated_low = activated.astype(jnp.bfloat16)
    result = middle + flat_dot(activated_low, w_down)
    block_output = result.astype(jnp.bfloat16).reshape(streams, local_rows, width)
    cot_flat = cotangent.reshape(tokens, width)
    grad_down = outer_dot(activated_low, cot_flat)
    d_activated = back_dot(cot_flat, w_down)
    d_hidden = gelu_back(d_activated)[0].astype(jnp.bfloat16)
    grad_up = outer_dot(normed_two, d_hidden)
    d_normed_two = back_dot(d_hidden, w_up)
    unused_two, norm_two_back = jax.vjp(layer_norm, middle, norm2_gain)
    d_middle_norm, grad_gain_two = norm_two_back(d_normed_two)
    d_middle = cot_flat.astype(jnp.float32) + d_middle_norm
    d_branch = d_middle.astype(jnp.bfloat16)
    grad_out = outer_dot(attended_low, d_branch)
    d_attended = back_dot(d_branch, w_out).astype(jnp.bfloat16)
    delta_rows = jnp.sum(
        (d_attended.astype(jnp.float32) * attended_flat).reshape(
            streams, local_rows, heads, head_width
        ),
        axis=-1,
    )
    lse_rows = log_total.transpose(0, 2, 1)
    delta_heads = delta_rows.transpose(0, 2, 1)
    d_attended_four = d_attended.reshape(streams, local_rows, heads, head_width)
    d_attended_rows = d_attended.reshape(streams, local_rows, width)

    def query_grads(state, block, first_row):
        key_block, value_block = block
        length = key_block.shape[1]
        allowed = key_mask(first_row, length)

        def query_compute(previous):
            key_four = key_block.reshape(streams, length, heads, head_width)
            value_four = value_block.reshape(streams, length, heads, head_width)
            scores = (
                jnp.einsum(
                    "bqhd,bkhd->bhqk", query_four, key_four, preferred_element_type=jnp.float32
                )
                * scale_factor
            )
            keeper = allowed[:, None, None, :]
            weights = jnp.where(keeper, jnp.exp(scores - log_total[..., None]), 0.0)
            d_weights = jnp.einsum(
                "bqhd,bkhd->bhqk", d_attended_four, value_four, preferred_element_type=jnp.float32
            )
            d_scores = (weights * (d_weights - delta_heads[..., None]) * scale_factor).astype(
                jnp.bfloat16
            )
            return previous + jnp.einsum(
                "bhqk,bkhd->bhqd", d_scores, key_four, preferred_element_type=jnp.float32
            )

        return lax.cond(jnp.any(allowed), query_compute, lambda previous: previous, state)

    zero_query = jnp.zeros((streams, heads, local_rows, head_width), jnp.float32)
    d_query_heads = over_blocks(
        zero_query,
        (
            lax.all_gather(keys_whole, "frame", axis=1, tiled=True),
            lax.all_gather(values_whole, "frame", axis=1, tiled=True),
        ),
        query_grads,
    )

    def make_fold(own_keys, own_values, rows_per_frame, lse_whole, delta_whole):
        key_count = own_keys.shape[1]
        own_key_four = own_keys.reshape(streams, key_count, heads, head_width)
        own_value_four = own_values.reshape(streams, key_count, heads, head_width)

        def work(state, block, first_row):
            query_block, grad_block, lse_block, delta_block = block
            length = query_block.shape[1]
            device = (first_row + jnp.arange(length, dtype=jnp.int32)) // rows_per_frame
            frames = frame_of(device)
            begins = lookup(frame_begin, frames)
            allowed = (my_frame[:, None] >= begins) & (my_frame[:, None] <= frames)

            def work_compute(previous):
                d_keys, d_values = previous
                query_block_four = query_block.reshape(streams, length, heads, head_width)
                grad_block_four = grad_block.reshape(streams, length, heads, head_width)
                scores = (
                    jnp.einsum(
                        "bqhd,bkhd->bhqk",
                        query_block_four,
                        own_key_four,
                        preferred_element_type=jnp.float32,
                    )
                    * scale_factor
                )
                keeper = allowed[:, None, :, None]
                weights = jnp.where(
                    keeper, jnp.exp(scores - lse_block.transpose(0, 2, 1)[..., None]), 0.0
                )
                d_values = d_values + jnp.einsum(
                    "bhqk,bqhd->bkhd",
                    weights.astype(jnp.bfloat16),
                    grad_block_four,
                    preferred_element_type=jnp.float32,
                )
                d_weights = jnp.einsum(
                    "bqhd,bkhd->bhqk",
                    grad_block_four,
                    own_value_four,
                    preferred_element_type=jnp.float32,
                )
                d_scores = (
                    weights * (d_weights - delta_block.transpose(0, 2, 1)[..., None]) * scale_factor
                ).astype(jnp.bfloat16)
                d_keys = d_keys + jnp.einsum(
                    "bhqk,bqhd->bkhd",
                    d_scores,
                    query_block_four,
                    preferred_element_type=jnp.float32,
                )
                return (d_keys, d_values)

            return lax.cond(jnp.any(allowed), work_compute, lambda previous: previous, state)

        def fold_queries(state, piece, start):
            length = piece[0].shape[1]
            return over_blocks(state, (piece[0], piece[1], lse_whole, delta_whole), work)

        return fold_queries

    lse_whole, delta_whole = (
        lax.all_gather(lse_rows, "frame", axis=1, tiled=True),
        lax.all_gather(delta_rows, "frame", axis=1, tiled=True),
    )
    zero_frame = jnp.zeros((streams, per_frame, heads, head_width), jnp.float32)
    frame_dkey, frame_dvalue = make_fold(
        keys_whole, values_whole, local_rows, lse_whole, delta_whole
    )(
        (zero_frame, zero_frame),
        (
            lax.all_gather(query, "frame", axis=1, tiled=True),
            lax.all_gather(d_attended_rows, "frame", axis=1, tiled=True),
        ),
        jnp.int32(0),
    )
    d_key_sum, d_value_sum = (
        lax.psum_scatter(
            frame_dkey.reshape(streams, per_frame, width).astype(jnp.bfloat16),
            "space",
            scatter_dimension=1,
            tiled=True,
        ).astype(jnp.float32),
        lax.psum_scatter(
            frame_dvalue.reshape(streams, per_frame, width).astype(jnp.bfloat16),
            "space",
            scatter_dimension=1,
            tiled=True,
        ).astype(jnp.float32),
    )
    unused_rope, rope_back = jax.vjp(rope_flat, jnp.zeros((tokens, width), jnp.float32))
    d_query_rows = d_query_heads.transpose(0, 2, 1, 3).reshape(streams, local_rows, width)
    d_query_low = rope_back(d_query_rows)[0].astype(jnp.bfloat16)
    d_key_low = rope_back(d_key_sum)[0].astype(jnp.bfloat16)
    d_value_low = d_value_sum.reshape(tokens, width).astype(jnp.bfloat16)
    grad_query = outer_dot(normed, d_query_low)
    grad_key = outer_dot(normed, d_key_low)
    grad_value = outer_dot(normed, d_value_low)
    d_normed = (
        back_dot(d_query_low, w_query) + back_dot(d_key_low, w_key) + back_dot(d_value_low, w_value)
    )
    unused_one, norm_one_back = jax.vjp(layer_norm, input_flat, norm1_gain)
    d_input_norm, grad_gain_one = norm_one_back(d_normed)
    grad_input = (d_middle + d_input_norm).reshape(streams, local_rows, width)
    summed = lax.psum(
        (
            grad_gain_one,
            grad_query,
            grad_key,
            grad_value,
            grad_out,
            grad_gain_two,
            grad_up,
            grad_down,
        ),
        ("frame", "space"),
    )
    return (
        block_output,
        grad_input,
        summed[0],
        summed[1],
        summed[2],
        summed[3],
        summed[4],
        summed[5],
        summed[6],
        summed[7],
    )


def solution(mesh):
    in_specs = (
        P(None, ("frame", "space"), None),
        P(),
        P(),
        P(),
        P(),
        P(),
        P(),
        P(),
        P(),
        P(),
        P(None, ("frame", "space"), None),
    )
    out_specs = (
        P(None, ("frame", "space"), None),
        P(None, ("frame", "space"), None),
        P(),
        P(),
        P(),
        P(),
        P(),
        P(),
        P(),
        P(),
    )
    return jax.shard_map(local, mesh=mesh, in_specs=in_specs, out_specs=out_specs, check_vma=False)
```

profile of v0, /device:TPU:0, one launch (start us, length us, event | category | flops | bytes accessed | tf_op | source)
XLA Modules:
  0.0 1234.3 jit_solution(14693150775180872070)
XLA Ops:
  28.9 5.5 fusion.97
  34.4 176.0 %all-gather.5.cloned.1.call-done = bf16[2,4096,768]{1,2,0:T(8,128)(2,1)} async-done(((bf16[2,256,768]{1,2,0:T(8,128)(2,1)}), bf16[2,4096,768]{1,2,0:T(8,128)(2,1)}) %all-gather.5.cloned.1.call-update) | async-done | bytes 12582928 | tf_op jit(solution)/shard_map/all_gather | solution.py:181
  210.4 186.2 %all-gather.7.cloned.1.call-done = bf16[2,4096,768]{1,2,0:T(8,128)(2,1)} async-done(((bf16[2,256,768]{1,2,0:T(8,128)(2,1)}), bf16[2,4096,768]{1,2,0:T(8,128)(2,1)}) %all-gather.7.cloned.1.call-update) | async-done | bytes 12582928 | tf_op jit(solution)/shard_map/all_gather | solution.py:182
  396.7 23.1 %while.57 = (s32[]{:T(128)}, f32[2,12,128]{2,1,0:T(8,128)S(1)}, f32[2,12,128]{2,1,0:T(8,128)S(1)}, f32[2,12,128,64]{2,3,1,0:T(8,128)S(1)}, s32[2,1]{0,1:T(1,128)...) while((s32[]{:T(128)}, f32[2,12,128]{2,1,0:T(8,128)S(1)}, ...), condition=%wide.region_13.14_spmd.clone, body=%wide.region_7.13_spmd.clone.sunk | while | flops 420374016 | bytes 30483760 | solution.py:75
  398.7 6.7 conditional.9
  426.1 7.4 fusion.50
  442.5 87.5 %all_gather.33 = f32[2,2048,12]{1,0,2:T(2,128)S(1)} all-gather(f32[2,128,12]{1,0,2:T(2,128)S(1)} %reduce_sum.216), channel_id=1, replica_groups=mesh['frame'=16,'space'=2] {'frame'}, dimensions={1}, use_global_device_ids=true | all-gather | bytes 208896 | tf_op jit(solution)/shard_map/all_gather | solution.py:321
  530.2 40.9 %all_gather.31 = f32[2,2048,12]{1,2,0:T(8,128)} all-gather(f32[2,128,12]{1,2,0:T(8,128)S(1)} %bitcast.221), channel_id=1, replica_groups=mesh['frame'=16,'space'=2] {'frame'}, dimensions={1}, use_global_device_ids=true | all-gather | bytes 208896 | tf_op jit(solution)/shard_map/all_gather | solution.py:320
  572.0 30.8 %while.58 = (s32[]{:T(128)}, f32[2,12,128,64]{2,3,1,0:T(8,128)}, s32[2,1]{0,1:T(1,128)}, bf16[2,4096,768]{1,2,0:T(8,128)(2,1)}, bf16[2,128,12,64]{1,3,2,0:T(8,12...) while((s32[]{:T(128)}, f32[2,12,128,64]{2,3,1,0:T(8,128)}, ...), condition=%wide.region_23.24_spmd.clone, body=%wide.region_19.23_spmd.clone.sunk | while | flops 615206400 | bytes 26033452 | solution.py:75
  574.0 14.5 %conditional.10 = (f32[2,12,128,64]{2,3,1,0:T(8,128)}) conditional(s32[]{:T(128)} %convert_element_type.250, f32[2,12,128,64]{2,3,1,0:T(8,128)} %get-tuple-element.1699, (pred[2,512]{1,0:T(4,128)(4,1)S(1)}, s32[]{:T(128)}, bf16[2,4096,768]{1,2,0:T(8,128)(2,1)}, bf16[2,128,12,64]{1,3,2,0:T(8,128)(2,1)S(1)}, f32[2,12,128]{2,1,0:T(8,128)S(1)}, ...), branch_computations={%region_21.21_spmd, %region_22.22_spmd} | conditional | flops 615186432 | bytes 26027082 | solution.py:246
  581.2 7.3 fusion.18
  602.9 32.2 %all-gather.11.cloned.1.call-done = bf16[2,2048,768]{1,2,0:T(8,128)(2,1)} async-done(((bf16[2,128,768]{1,2,0:T(8,128)(2,1)}), bf16[2,2048,768]{1,2,0:T(8,128)(2,1)}) %all-gather.11.cloned.1.call-update) | async-done | bytes 6291472 | tf_op jit(solution)/shard_map/all_gather | solution.py:330
  637.7 86.4 %while.59 = (s32[]{:T(128)}, f32[2,256,12,64]{1,3,2,0:T(8,128)}, f32[2,256,12,64]{1,3,2,0:T(8,128)}, s32[2,16]{1,0:T(2,128)S(1)}, bf16[2,2048,768]{1,2,0:T(8,128...) while((s32[]{:T(128)}, f32[2,256,12,64]{1,3,2,0:T(8,128)}, ...), condition=%wide.region_29.30_spmd.clone, body=%wide.region_24.29_spmd.clone.sunk | while | flops 1646070272 | bytes 115180016 | solution.py:75
  639.1 20.2 %conditional.11 = ((f32[2,256,12,64]{1,3,2,0:T(8,128)}, f32[2,256,12,64]{1,3,2,0:T(8,128)})) conditional(s32[]{:T(128)} %convert_element_type.251, (f32[2,256,12,64]{1,3,2,0:T(8,128)}, f32[2,256,12,64]{1,3,2,0:T(8,128)}) %tuple.222, (pred[2,512]{1,0:T(4,128)(4,1)S(1)}, s32[]{:T(128)}, bf16[2,2048,768]{1,2,0:T(8,128)(2,1)}, ...), branch_computations={%region_27.27_spmd, %region_28.28_spmd} | conditional | flops 1646002176 | bytes 115165296 | solution.py:311
  644.2 5.3 bitcast_add_fusion
  649.5 9.8 bitcast_add_fusion.1
  660.8 20.2 %conditional.11 = ((f32[2,256,12,64]{1,3,2,0:T(8,128)}, f32[2,256,12,64]{1,3,2,0:T(8,128)})) conditional(s32[]{:T(128)} %convert_element_type.251, (f32[2,256,12,64]{1,3,2,0:T(8,128)}, f32[2,256,12,64]{1,3,2,0:T(8,128)}) %tuple.222, (pred[2,512]{1,0:T(4,128)(4,1)S(1)}, s32[]{:T(128)}, bf16[2,2048,768]{1,2,0:T(8,128)(2,1)}, ...), branch_computations={%region_27.27_spmd, %region_28.28_spmd} | conditional | flops 1646002176 | bytes 115165296 | solution.py:311
  665.8 5.3 bitcast_add_fusion
  671.1 9.8 bitcast_add_fusion.1
  682.4 20.2 %conditional.11 = ((f32[2,256,12,64]{1,3,2,0:T(8,128)}, f32[2,256,12,64]{1,3,2,0:T(8,128)})) conditional(s32[]{:T(128)} %convert_element_type.251, (f32[2,256,12,64]{1,3,2,0:T(8,128)}, f32[2,256,12,64]{1,3,2,0:T(8,128)}) %tuple.222, (pred[2,512]{1,0:T(4,128)(4,1)S(1)}, s32[]{:T(128)}, bf16[2,2048,768]{1,2,0:T(8,128)(2,1)}, ...), branch_computations={%region_27.27_spmd, %region_28.28_spmd} | conditional | flops 1646002176 | bytes 115165296 | solution.py:311
  687.4 5.3 bitcast_add_fusion
  692.7 9.8 bitcast_add_fusion.1
  704.0 20.2 %conditional.11 = ((f32[2,256,12,64]{1,3,2,0:T(8,128)}, f32[2,256,12,64]{1,3,2,0:T(8,128)})) conditional(s32[]{:T(128)} %convert_element_type.251, (f32[2,256,12,64]{1,3,2,0:T(8,128)}, f32[2,256,12,64]{1,3,2,0:T(8,128)}) %tuple.222, (pred[2,512]{1,0:T(4,128)(4,1)S(1)}, s32[]{:T(128)}, bf16[2,2048,768]{1,2,0:T(8,128)(2,1)}, ...), branch_computations={%region_27.27_spmd, %region_28.28_spmd} | conditional | flops 1646002176 | bytes 115165296 | solution.py:311
  709.0 5.3 bitcast_add_fusion
  714.3 9.8 bitcast_add_fusion.1
  730.9 6.8 fusion.85
  737.7 6.0 fusion.87
  755.4 4.1 reduce-scatter.5.cloned.1.call-done
  762.4 6.1 fusion.51
  771.4 42.7 %all-reduce.4 = (f32[768]{0:T(1024)}, f32[768]{0:T(1024)}) all-reduce(f32[768]{0:T(1024)S(1)} %get-tuple-element.1276, f32[768]{0:T(1024)S(1)} %copy-done.52), channel_id=1, replica_groups=mesh['frame'=16,'space'=2] {'frame','space'}, use_global_device_ids=true, to_apply=%region_35.36 | all-reduce | flops 1536 | bytes 12288 | tf_op jit(solution)/shard_map/psum | solution.py:362
  815.4 388.9 %all-reduce.8.cloned.1.call-done = (f32[768,768]{1,0:T(8,128)}, f32[768,768]{1,0:T(8,128)}, f32[768,768]{1,0:T(8,128)}, f32[768,768]{1,0:T(8,128)}, f32[768,3072]{1,0:T(8,128)}, /*index=5*/f32[3072,768]{1,0:T(8,128)}) async-done(((f32[768,768]{1,0:T(8,128)}, f32[768,768]{1,0:T(8,128)}, f32[768,768]{1,0:T(8,128)}, f32[768,768]{1,0:T(8,128)}, f32[768,3072]{1,0:T(8,128)}, /*index=5*/f32[3072,768]{1,0:T(8,128)}), ...) | async-done | bytes 28311568 | tf_op jit(solution)/shard_map/psum | solution.py:362
  1214.2 9.3 copy.164
  (333 shorter events, 137.7 us)
Async XLA Ops:
  7.2 416.7 %copy-start = (bf16[768,768]{1,0:T(8,128)(2,1)S(1)}, bf16[768,768]{1,0:T(8,128)(2,1)}, u32[]{:S(2)}) copy-start(bf16[768,768]{1,0:T(8,128)(2,1)} %param.28) | copy-start | bytes 3538948
  7.2 8.3 copy-start.6
  7.2 8.3 copy-start.35
  7.2 203.2 %all-gather.5.cloned.1.call-start = ((), (), s32[]{:S(2)}) async-start(), calls=%async_computation.2 | async-start | bytes 13369344 | tf_op jit(solution)/shard_map/all_gather | solution.py:181
  9.0 19.2 %copy-start.37 = (s32[2,16]{1,0:T(2,128)}, s32[2,16]{1,0:T(2,128)S(1)}, u32[]{:S(2)}) copy-start(s32[2,16]{1,0:T(2,128)S(1)} %get-tuple-element.1650) | copy-start | bytes 388
  10.3 12.2 copy-start.39
  11.5 11.0 copy-start.45
  22.4 6.5 copy-start.16
  22.4 374.1 %all-gather.7.cloned.1.call-start = ((), (), s32[]{:S(2)}) async-start(), calls=%async_computation.3 | async-start | bytes 13369344 | tf_op jit(solution)/shard_map/all_gather | solution.py:182
  27.3 575.6 %all-gather.9.cloned.1.call-start = ((), (), s32[]{:S(2)}) async-start(), calls=%async_computation.4 | async-start | bytes 6684672 | tf_op jit(solution)/shard_map/all_gather | solution.py:329
  28.0 607.1 %all-gather.11.cloned.1.call-start = ((), (), s32[]{:S(2)}) async-start(), calls=%async_computation.5 | async-start | bytes 6684672 | tf_op jit(solution)/shard_map/all_gather | solution.py:330
  28.9 367.8 %copy-start.3 = (bf16[2,128,12,64]{1,3,2,0:T(8,128)(2,1)S(1)}, bf16[2,128,12,64]{1,3,2,0:T(8,128)(2,1)}, u32[]{:S(2)}) copy-start(bf16[2,128,12,64]{1,3,2,0:T(8,128)(2,1)} %get-tuple-element.1690) | copy-start | bytes 1179652
  423.9 9.6 slice-start.3
  424.5 11.2 copy-start.10
  424.5 11.2 copy-start.41
  426.1 9.6 copy-start.48
  426.1 7.4 slice-start.4
  439.5 307.1 %reduce-scatter.7.cloned.1.call-start = ((), (), s32[]{:S(2)}) async-start(), calls=%async_computation.7 | async-start | bytes 1179648
  439.7 90.5 %copy-start.32 = (f32[2,12,128]{2,1,0:T(8,128)S(1)}, f32[2,12,128]{2,1,0:T(8,128)}, u32[]{:S(2)}) copy-start(f32[2,12,128]{2,1,0:T(8,128)} %copy-done.31) | copy-start | bytes 36868
  602.9 34.9 %copy-start.5 = (bf16[2,256,768]{1,2,0:T(8,128)(2,1)S(1)}, bf16[2,256,768]{1,2,0:T(8,128)(2,1)}, u32[]{:S(2)}) copy-start(bf16[2,256,768]{1,2,0:T(8,128)(2,1)} %all_gather.26) | copy-start | bytes 2359300
  602.9 34.9 %copy-start.38 = (s32[2,16]{1,0:T(2,128)S(1)}, s32[2,16]{1,0:T(2,128)}, u32[]{:S(2)}) copy-start(s32[2,16]{1,0:T(2,128)} %copy-done.37) | copy-start | bytes 388
  643.3 6.3 copy-start.2
  664.9 6.3 copy-start.2
  727.5 31.9 %reduce-scatter.5.cloned.1.call-start = ((), (), s32[]{:S(2)}) async-start(), calls=%async_computation.6 | async-start | bytes 1179648 | tf_op jit(solution)/shard_map/reduce_scatter | solution.py:341
  730.8 6.9 copy-start.17
  730.9 6.9 copy-start.18
  746.4 457.9 %all-reduce.8.cloned.1.call-start = ((), (), s32[]{:S(2)}) async-start(), calls=%async_computation.8 | async-start | bytes 56623104 | tf_op jit(solution)/shard_map/psum | solution.py:362
  770.3 43.9 %copy-start.15 = (f32[256,768]{1,0:T(8,128)S(1)}, f32[256,768]{1,0:T(8,128)}, u32[]{:S(2)}) copy-start(f32[256,768]{1,0:T(8,128)} %copy-done.14) | copy-start | bytes 2359300
  770.3 43.9 %copy-start.51 = (f32[256]{0:T(256)S(1)}, f32[256]{0:T(256)}, u32[]{:S(2)}) copy-start(f32[256]{0:T(256)} %copy-done.50) | copy-start | bytes 3076
  1212.7 10.7 slice-start
  1214.2 9.3 slice-start.1
  1214.2 9.3 slice-start.2
  (39 other events, 106.2 us)
Sparse Core Ops, SparseCore 0:
  22.6 187.7 all-gather.4
  213.1 183.3 all-gather.6
  399.8 115.8 all-gather.8
  518.8 116.2 all-gather.10
  727.6 12.8 reduce-scatter.6
  746.5 12.8 reduce-scatter.4
  767.0 437.2 all-reduce.7
where the time goes:
time: 1240 us; the launch traced here: 1230 us
  waiting for transfers between devices  788 us (64%)
  blocking collectives  176 us (14%)
  matrix products  133 us (11%)
  local copies, waits for them, and re-layouts  64.9 us (5%)
  other arithmetic  42.3 us (3%)
  between operations  15.2 us (1%)
  loops' own time  14.2 us (1%)
    psum x1, waiting for transfers between devices, local(): lax.psum((grad_gain_one, grad_query, grad_key, grad_value, grad_out, grad...  389 us
    all_gather x1, waiting for transfers between devices, local(): lax.all_gather(values_whole, 'frame', axis=1, tiled=True)  186 us
    all_gather x1, waiting for transfers between devices, local(): lax.all_gather(keys_whole, 'frame', axis=1, tiled=True)  176 us
    all_gather x1, blocking collectives, local(): lax.all_gather(delta_rows, 'frame', axis=1, tiled=True)  87.5 us
    psum x1, blocking collectives, local(): lax.psum((grad_gain_one, grad_query, grad_key, grad_value, grad_out, grad...  42.7 us
    all_gather x1, blocking collectives, local(): lax.all_gather(lse_rows, 'frame', axis=1, tiled=True)  40.9 us
    dot_general x4, matrix products, work_compute(): jnp.einsum('bhqk,bqhd->bkhd', d_scores, query_block_four, preferred_eleme...  39.3 us
    unnamed x126, local copies, waits for them, and re-layouts  35.1 us
  transfers between devices with their start and end apart: 7, of which 5 were waited for; matrix products, arithmetic and copies ran while one was open for 9% of the time, Pallas kernels for 0%

commit v1 on v0

v1 whole, which is shorter than its diff:
```python
import functools
import math

import jax
import jax.numpy as jnp
from jax import lax
from jax.experimental import pallas as pl
from jax.experimental.pallas import tpu as pltpu
from jax.sharding import PartitionSpec as P

HEADS = 12
HEAD_DIM = 64

NEG=-1e30
def dotT(a,b,ca,cb):
    return lax.dot_general(a,b,(((ca,),(cb,)),((),())),preferred_element_type=jnp.float32)

def fwd_kernel(lo_ref, r_ref, o_ref, lse_ref, kn, qt, vt, s_buf, *, nf, rows, G):
    spc = r_ref.shape[0]//nf
    tpf = spc*rows
    for_ = r_ref.shape[0]
    def prep(d, _):
        kT = r_ref[d, 64:128, :]
        kn[pl.ds(pl.multiple_of(d*rows,rows), rows), :] = kT.T
        return 0
    lax.fori_loop(0, for_, prep, 0)
    def prep2(f, _):
        qt[f] = jnp.concatenate([r_ref[f*spc+j,0:64,:] for j in range(spc)],axis=1)
        vt[f] = jnp.concatenate([r_ref[f*spc+j,128:192,:] for j in range(spc)],axis=1)
        return 0
    lax.fori_loop(0, nf, prep2, 0)
    def one_frame(f, _):
        lo = lo_ref[f]
        q = qt[f]
        n = (f - lo)//G
        def scores(g0, cnt):
            return dotT(kn[pl.ds(pl.multiple_of(g0*tpf,tpf), cnt*tpf), :], q, 1, 0)
        def step(g0, cnt, s, state):
            m, l, o = state
            mn = jnp.maximum(m, jnp.max(s, axis=0, keepdims=True))
            a = jnp.exp(m-mn)
            p = jnp.exp(s-mn)
            l = l*a + jnp.sum(p,axis=0,keepdims=True)
            pb = p.astype(jnp.bfloat16)
            o = o*a
            for j in range(cnt):
                o = o + dotT(vt[g0+j], pb[j*tpf:(j+1)*tpf], 1, 0)
            return mn,l,o
        state=(jnp.full((1,tpf),NEG,jnp.float32),jnp.zeros((1,tpf),jnp.float32),jnp.zeros((64,tpf),jnp.float32))
        def body(i, st):
            g0 = lo+i*G
            return step(g0, G, scores(g0,G), st)
        state=lax.fori_loop(0,n,body,state)
        def tail(i, st):
            g0 = lo+n*G+i
            return step(g0,1,scores(g0,1),st)
        state=lax.fori_loop(0, f-lo-n*G+1, tail, state)
        m,l,o=state
        o = o/l
        for j in range(spc):
            o_ref[f*spc+j] = o[:,j*rows:(j+1)*rows]
        lse_ref[f] = m+jnp.log(l)
        return 0
    lax.fori_loop(0,nf,one_frame,0)

def attn_fwd(lo, r, nf, G=4):
    nd,_,rows=r.shape
    tpf=nd//nf*rows
    return pl.pallas_call(functools.partial(fwd_kernel,nf=nf,rows=rows,G=G),
        out_shape=(jax.ShapeDtypeStruct((nd,64,rows),jnp.float32),jax.ShapeDtypeStruct((nf,1,tpf),jnp.float32)),
        in_specs=[pl.BlockSpec(memory_space=pltpu.SMEM),pl.BlockSpec(memory_space=pltpu.VMEM)],
        out_specs=(pl.BlockSpec(memory_space=pltpu.VMEM),)*2,
        scratch_shapes=[pltpu.VMEM((nd*rows,64),jnp.bfloat16),pltpu.VMEM((nf,64,tpf),jnp.bfloat16),pltpu.VMEM((nf,64,tpf),jnp.bfloat16),pltpu.VMEM((G*tpf,tpf),jnp.float32)],
        compiler_params=pltpu.CompilerParams(vmem_limit_bytes=48*2**20),
        name="attn_fwd")(lo,r)

def bwd_kernel(hi_ref, r_ref, do_ref, o_ref, lse_ref, d_ref, kn, vn, qt, qn, don, dot_, dq, delta, *, nf, rows):
    nd=r_ref.shape[0]; spc=nd//nf; tpf=spc*rows
    def prep(f,_):
        for j in range(spc):
            d=f*spc+j
            blk=r_ref[d]
            sl=pl.ds(pl.multiple_of(d*rows,rows),rows)
            kn[sl,:]=blk[64:128].T
            vn[sl,:]=blk[128:192].T
            qn[sl,:]=blk[0:64].T
            don[sl,:]=do_ref[d].T
        qt[f]=jnp.concatenate([r_ref[f*spc+j,0:64,:] for j in range(spc)],axis=1)
        dd=jnp.concatenate([do_ref[f*spc+j] for j in range(spc)],axis=1)
        oo=jnp.concatenate([o_ref[f*spc+j] for j in range(spc)],axis=1)
        dot_[f]=dd
        delta[f]=jnp.sum(dd.astype(jnp.float32)*oo,axis=0,keepdims=True)
        dq[f]=jnp.zeros((64,tpf),jnp.float32)
        return 0
    lax.fori_loop(0,nf,prep,0)
    def one_key(kf,_):
        sl=pl.ds(pl.multiple_of(kf*tpf,tpf),tpf)
        k=kn[sl,:]; v=vn[sl,:]
        kT=jnp.concatenate([r_ref[kf*spc+j,64:128,:] for j in range(spc)],axis=1)
        def body(f, st):
            dk,dv=st
            qsl=pl.ds(pl.multiple_of(f*tpf,tpf),tpf)
            s=dotT(k,qt[f],1,0)
            p=jnp.exp(s-lse_ref[f])
            dp=dotT(v,dot_[f],1,0)
            ds=(p*(dp-delta[f])).astype(jnp.bfloat16)
            dv=dv+dotT(p.astype(jnp.bfloat16),don[qsl,:],1,0)
            dk=dk+dotT(ds,qn[qsl,:],1,0)
            dq[f]=dq[f]+dotT(kT,ds,1,0)
            return dk,dv
        z=jnp.zeros((tpf,64),jnp.float32)
        dk,dv=lax.fori_loop(kf,hi_ref[kf],body,(z,z))
        dkT=dk.T; dvT=dv.T
        for j in range(spc):
            d_ref[kf*spc+j,64:128,:]=dkT[:,j*rows:(j+1)*rows].astype(jnp.bfloat16)
            d_ref[kf*spc+j,128:192,:]=dvT[:,j*rows:(j+1)*rows].astype(jnp.bfloat16)
        return 0
    lax.fori_loop(0,nf,one_key,0)
    def fin(f,_):
        x=dq[f]
        for j in range(spc):
            d_ref[f*spc+j,0:64,:]=x[:,j*rows:(j+1)*rows].astype(jnp.bfloat16)
        return 0
    lax.fori_loop(0,nf,fin,0)

def attn_bwd(hi, r, do, o, lse, nf):
    nd,_,rows=r.shape; tpf=nd//nf*rows; n=nd*rows
    V=pltpu.VMEM
    return pl.pallas_call(functools.partial(bwd_kernel,nf=nf,rows=rows),
        out_shape=jax.ShapeDtypeStruct((nd,192,rows),jnp.bfloat16),
        in_specs=[pl.BlockSpec(memory_space=pltpu.SMEM)]+[pl.BlockSpec(memory_space=V)]*4,
        out_specs=pl.BlockSpec(memory_space=V),
        scratch_shapes=[V((n,64),jnp.bfloat16)]*2+[V((nf,64,tpf),jnp.bfloat16)]+[V((n,64),jnp.bfloat16)]*2+[V((nf,64,tpf),jnp.bfloat16),V((nf,64,tpf),jnp.float32),V((nf,1,tpf),jnp.float32)],
        compiler_params=pltpu.CompilerParams(vmem_limit_bytes=48*2**20),
        name="attn_bwd")(hi,r,do,o,lse)


def layer_norm(values, gain_vector):
    average = jnp.mean(values, axis=-1, keepdims=True)
    centred = values - average
    spread = jnp.mean(centred * centred, axis=-1, keepdims=True)
    return centred * lax.rsqrt(spread + 1e-05) * gain_vector


def frame_tables(clip_frames, frame_count):
    clip_ends = jnp.cumsum(clip_frames, axis=1, dtype=jnp.int32)
    clip_begins = clip_ends - clip_frames
    frame_index = jnp.arange(frame_count, dtype=jnp.int32)
    inside = (frame_index[None, :, None] >= clip_begins[:, None, :]) & (
        frame_index[None, :, None] < clip_ends[:, None, :]
    )
    begin = jnp.sum(jnp.where(inside, clip_begins[:, None, :], 0), axis=2, dtype=jnp.int32)
    end = jnp.sum(jnp.where(inside, clip_ends[:, None, :], 0), axis=2, dtype=jnp.int32)
    return begin, end


def dot(left, right, left_dim, right_dim):
    return lax.dot_general(
        left,
        right,
        (((left_dim,), (right_dim,)), ((), ())),
        preferred_element_type=jnp.float32,
    )


def turn(values, cosine, sine, sign):
    first, second = values[:, 0], values[:, 1]
    return jnp.stack(
        [first * cosine - sign * second * sine, second * cosine + sign * first * sine], axis=1
    )


def local(
    block_input,
    norm1_gain,
    w_query,
    w_key,
    w_value,
    w_out,
    norm2_gain,
    w_up,
    w_down,
    clip_frames,
    cotangent,
):
    streams, rows, width = block_input.shape
    heads, head_width = HEADS, HEAD_DIM
    half = head_width // 2
    frames = lax.axis_size("frame")
    spaces = lax.axis_size("space")
    devices = frames * spaces
    pairs = streams * heads
    per_frame = rows * spaces
    tokens = streams * rows
    axes = ("frame", "space")
    frame_place = lax.axis_index("frame")
    space_place = lax.axis_index("space")
    low = jnp.bfloat16

    begin, end = frame_tables(clip_frames, frames)
    frame_ids = jnp.arange(frames, dtype=jnp.int32)
    my_time = jnp.sum(
        jnp.where(frame_ids[None, :] == frame_place, frame_ids[None, :] - begin, 0), axis=1
    )
    within = space_place * rows + jnp.arange(rows, dtype=jnp.int32)
    position = (my_time[:, None] * per_frame + within[None, :]).astype(jnp.float32)
    frequency = jnp.exp(
        jnp.arange(half, dtype=jnp.float32) * (-2.0 * math.log(10000.0) / head_width)
    )
    angles = frequency[:, None, None] * position[None]
    cosine, sine = jnp.cos(angles), jnp.sin(angles)

    mine = frame_place * spaces + space_place
    my_stream = jnp.minimum(mine // heads, streams - 1)
    idle = mine >= pairs
    picked = jnp.arange(streams, dtype=jnp.int32)[:, None] == my_stream
    lo = jnp.where(idle, frame_ids, jnp.sum(jnp.where(picked, begin, 0), axis=0))
    hi = jnp.where(idle, frame_ids, jnp.sum(jnp.where(picked, end, 0), axis=0))

    def to_heads(parts):
        whole = jnp.stack(parts, axis=1).transpose(3, 0, 1, 2, 4)
        whole = whole.reshape(pairs, len(parts) * head_width, rows)
        whole = jnp.pad(whole, ((0, devices - pairs), (0, 0), (0, 0)))
        return lax.all_to_all(whole, axes, 0, 0, tiled=True)

    def to_tokens(whole, count):
        back = lax.all_to_all(whole, axes, 0, 0, tiled=True)[:pairs]
        back = back.reshape(streams, heads, count, head_width, rows)
        return back.transpose(2, 1, 3, 0, 4)

    input_flat = block_input.astype(jnp.float32).reshape(tokens, width)
    normed = layer_norm(input_flat, norm1_gain).astype(low)

    def project(weight):
        return dot(weight, normed, 0, 1)

    def rope(value):
        value = value.reshape(heads, 2, half, streams, rows)
        return turn(value, cosine, sine, 1.0).reshape(heads, head_width, streams, rows)

    scale = 1.0 / math.sqrt(head_width)
    query = (rope(project(w_query)) * scale).astype(low)
    key = rope(project(w_key)).astype(low)
    value = project(w_value).astype(low).reshape(heads, head_width, streams, rows)
    packed = to_heads([query, key, value])
    attended_own, lse = attn_fwd(lo, packed, frames)
    attended = to_tokens(attended_own.astype(low), 1)[0].reshape(width, tokens)

    middle = input_flat + dot(attended, w_out, 0, 0)
    normed_two = layer_norm(middle, norm2_gain).astype(low)
    hidden = dot(normed_two, w_up, 1, 0)
    activated, gelu_back = jax.vjp(lambda inner: jax.nn.gelu(inner, approximate=True), hidden)
    activated_low = activated.astype(low)
    block_output = (middle + dot(activated_low, w_down, 1, 0)).astype(low)
    cot_flat = cotangent.reshape(tokens, width)
    d_activated = dot(cot_flat, w_down, 1, 1)
    d_hidden = gelu_back(d_activated)[0].astype(low)
    d_normed_two = dot(d_hidden, w_up, 1, 1)
    unused_two, norm_two_back = jax.vjp(layer_norm, middle, norm2_gain)
    d_middle_norm, grad_gain_two = norm_two_back(d_normed_two)
    d_middle = cot_flat.astype(jnp.float32) + d_middle_norm
    d_branch = d_middle.astype(low)
    d_attended = dot(w_out, d_branch, 1, 1).astype(low)
    d_own = to_heads([d_attended.reshape(heads, head_width, streams, rows)])

    grad_down = dot(activated_low, cot_flat, 0, 0)
    grad_up = dot(normed_two, d_hidden, 0, 0)
    grad_out = dot(attended, d_branch, 1, 0)
    early = lax.psum((grad_down.astype(low), grad_up.astype(low), grad_out.astype(low)), axes)

    grads_own = attn_bwd(hi, packed, d_own, attended_own, lse, frames)
    d_three = to_tokens(grads_own, 3)

    def rope_back(value):
        value = value.astype(jnp.float32).reshape(heads, 2, half, streams, rows)
        return turn(value, cosine, sine, -1.0).reshape(width, tokens)

    d_query = (rope_back(d_three[0]) * scale).astype(low)
    d_key = rope_back(d_three[1]).astype(low)
    d_value = d_three[2].reshape(width, tokens)
    grad_query = dot(normed, d_query, 0, 1)
    grad_key = dot(normed, d_key, 0, 1)
    grad_value = dot(normed, d_value, 0, 1)
    d_normed = (
        dot(d_query, w_query, 0, 1) + dot(d_key, w_key, 0, 1) + dot(d_value, w_value, 0, 1)
    )
    unused_one, norm_one_back = jax.vjp(layer_norm, input_flat, norm1_gain)
    d_input_norm, grad_gain_one = norm_one_back(d_normed)
    grad_input = (d_middle + d_input_norm).reshape(streams, rows, width)
    late = lax.psum(
        (grad_query.astype(low), grad_key.astype(low), grad_value.astype(low)), axes
    )
    gains = lax.psum((grad_gain_one, grad_gain_two), axes)
    wide = lambda member: member.astype(jnp.float32)
    return (
        block_output.reshape(streams, rows, width),
        grad_input,
        gains[0],
        wide(late[0]),
        wide(late[1]),
        wide(late[2]),
        wide(early[2]),
        gains[1],
        wide(early[1]),
        wide(early[0]),
    )


def solution(mesh):
    spread = P(None, ("frame", "space"), None)
    in_specs = (spread,) + (P(),) * 9 + (spread,)
    out_specs = (spread, spread) + (P(),) * 8
    return jax.shard_map(local, mesh=mesh, in_specs=in_specs, out_specs=out_specs, check_vma=False)
```

time: 1240 us -> 554 us (0.45)
  waiting for transfers between devices: 788 us -> 289 us
  blocking collectives: 176 us -> 40.6 us
  matrix products: 133 us -> 45.8 us
  Pallas kernels: 0 us -> 65.3 us
  local copies, waits for them, and re-layouts: 64.9 us -> 20.4 us
  starting transfers between devices: 0.63 us -> 41.1 us
  loops' own time: 14.2 us -> 0 us
    all_gather x4 -> x0, waiting for transfers between devices: 394 us -> none  [the longest x1 186 us: local(): lax.all_gather(values_whole, 'frame', axis=1, tiled=True)]
    psum x1, waiting for transfers between devices: 389 us -> 201 us  [local(): lax.psum((grad_query.astype(low), grad_key.astype(low), grad_value.astype...]
    all_gather x4 -> x0, blocking collectives: 133 us -> none  [the longest x1 87.5 us: local(): lax.all_gather(delta_rows, 'frame', axis=1, tiled=True)]
    all_to_all x0 -> x4, waiting for transfers between devices: none -> 88 us  [the longest x2 53.2 us: to_heads(): return lax.all_to_all(whole, axes, 0, 0, tiled=True)]
    dot_general x34 -> x18, matrix products: 133 us -> 45.8 us  [dot(): lax.dot_general(left, right, (((left_dim,), (right_dim,)), ((), ())), pre...]
    pallas_call x0 -> x2, Pallas kernels: none -> 65.3 us  [the longest x1 37.7 us: attn_bwd(): pl.pallas_call(functools.partial(bwd_kernel, nf=nf, rows=rows), out_shape...]
    all_to_all x0 -> x4, starting transfers between devices: none -> 40.9 us  [the longest x2 30.5 us: to_tokens(): back = lax.all_to_all(whole, axes, 0, 0, tiled=True)[:pairs]]
    unnamed x126 -> x112, local copies, waits for them, and re-layouts: 35.1 us -> 5.34 us
  transfers between devices with their start and end apart: 7 -> 5, of which waited for: 5 -> 5; matrix products, arithmetic and copies ran while one was open for 9% -> 5% of each run, Pallas kernels for 0% -> 0%
where the time goes in v1:
time: 554 us; the launch traced here: 553 us
  waiting for transfers between devices  289 us (52%)
  Pallas kernels  65.3 us (12%)
  matrix products  45.8 us (8%)
  starting transfers between devices  41.1 us (7%)
  blocking collectives  40.6 us (7%)
  other arithmetic  35.1 us (6%)
  local copies, waits for them, and re-layouts  20.4 us (4%)
  between operations  14.9 us (3%)
    psum x1, waiting for transfers between devices, local(): lax.psum((grad_query.astype(low), grad_key.astype(low), grad_value.astype...  201 us
    all_to_all x2, waiting for transfers between devices, to_heads(): return lax.all_to_all(whole, axes, 0, 0, tiled=True)  53.2 us
    dot_general x18, matrix products, dot(): lax.dot_general(left, right, (((left_dim,), (right_dim,)), ((), ())), pre...  45.8 us
    psum x1, blocking collectives, local(): gains = lax.psum((grad_gain_one, grad_gain_two), axes)  40.6 us
    pallas_call x1, Pallas kernels, attn_bwd(): pl.pallas_call(functools.partial(bwd_kernel, nf=nf, rows=rows), out_shape...  37.7 us
    all_to_all x2, waiting for transfers between devices, to_tokens(): back = lax.all_to_all(whole, axes, 0, 0, tiled=True)[:pairs]  34.8 us
    all_to_all x2, starting transfers between devices, to_tokens(): back = lax.all_to_all(whole, axes, 0, 0, tiled=True)[:pairs]  30.5 us
    pallas_call x1, Pallas kernels, attn_fwd(): pl.pallas_call(functools.partial(fwd_kernel, nf=nf, rows=rows, G=G), out_...  27.6 us
  transfers between devices with their start and end apart: 5, of which 5 were waited for; matrix products, arithmetic and copies ran while one was open for 5% of the time, Pallas kernels for 0%

profile of v1, /device:TPU:0, one launch (start us, length us, event | category | flops | bytes accessed | tf_op | source)
XLA Modules:
  0.0 552.7 jit_solution(11901020824253969305)
XLA Ops:
  14.0 1.7 fusion.8
  18.1 1.5 copy.38
  22.2 1.4 copy.37
  27.1 2.0 maximum_bitcast_fusion
  30.8 7.3 %all-to-all-start = ((bf16[32,192,128]{2,1,0:T(8,128)(2,1)}), bf16[32,192,128]{2,1,0:T(8,128)(2,1)S(1)}, u32[]{:S(2)}, u32[]{:S(2)}) async-start(bf16[32,192,128]{2,1,0:T(8,128)(2,1)} %pad.8), calls=%async_computation | async-start | bytes 3145728 | tf_op jit(solution)/shard_map/all_to_all | solution.py:224
  38.1 37.7 %all-to-all-done.r_ref = bf16[32,192,128]{2,1,0:T(8,128)(2,1)S(1)} async-done(((bf16[32,192,128]{2,1,0:T(8,128)(2,1)}), bf16[32,192,128]{2,1,0:T(8,128)(2,1)S(1)}, u32[]{:S(2)}, u32[]{:S(2)}) %all-to-all-start) | async-done | bytes 1572896 | tf_op jit(solution)/shard_map/all_to_all | solution.py:224
  75.8 27.6 %attn_fwd.1 = (f32[32,64,128]{2,1,0:T(8,128)S(1)}, f32[16,1,256]{2,1,0:T(1,128)S(1)}) custom-call(s32[16]{0:T(128)S(1)} %broadcast_select_fusion.1.lo_ref, bf16[32,192,128]{2,1,0:T(8,128)(2,1)S(1)} %all-to-all-done.r_ref), custom_call_target="tpu_custom_call" | custom-call | tf_op jit(solution)/shard_map/attn_fwd/pallas_call | solution.py:69
  105.2 10.6 %all-to-all-start.1 = ((bf16[32,64,128]{2,1,0:T(8,128)(2,1)}), bf16[32,64,128]{2,1,0:T(8,128)(2,1)}, u32[]{:S(2)}, u32[]{:S(2)}) async-start(bf16[32,64,128]{2,1,0:T(8,128)(2,1)} %convert_element_type.165), calls=%async_computation.1 | async-start | bytes 1048576 | tf_op jit(solution)/shard_map/all_to_all | solution.py:227
  115.8 5.5 fusion.39
  121.3 9.9 %all-to-all-done.1 = bf16[32,64,128]{2,1,0:T(8,128)(2,1)} async-done(((bf16[32,64,128]{2,1,0:T(8,128)(2,1)}), bf16[32,64,128]{2,1,0:T(8,128)(2,1)}, u32[]{:S(2)}, u32[]{:S(2)}) %all-to-all-start.1) | async-done | bytes 524320 | tf_op jit(solution)/shard_map/all_to_all | solution.py:227
  133.8 7.7 %fusion.6 = (bf16[256,3072]{1,0:T(8,128)(2,1)S(1)}, f32[256,3072]{1,0:T(8,128)}) fusion(f32[256,3072]{1,0:T(8,128)S(1)} %copy-done.23, bf16[768,3072]{1,0:T(8,128)(2,1)} %param.18, f32[256,768]{1,0:T(8,128)S(1)} %get-tuple-element.52, f32[768]{0:T(1024)S(1)} %copy-done.33, f32[256]{0:T(256)S(1)} %fusion.31, f32[256]{0:T(256)S(1)} %broadcast_multiply_fusion.1), kind=kOutput, calls=%fused_computation.10 | convolution fusion | flops 1224474624 | bytes 13374464 | tf_op jit(solution)/shard_map/dot_general | solution.py:158
  141.4 2.3 multiply_reduce_fusion
  150.3 3.1 all-to-all-start.2
  153.4 15.5 %all-to-all-done.2.do_ref = bf16[32,64,128]{2,1,0:T(8,128)(2,1)S(1)} async-done(((bf16[32,64,128]{2,1,0:T(8,128)(2,1)}), bf16[32,64,128]{2,1,0:T(8,128)(2,1)S(1)}, u32[]{:S(2)}, u32[]{:S(2)}) %all-to-all-start.2) | async-done | bytes 524320 | tf_op jit(solution)/shard_map/all_to_all | solution.py:224
  169.0 37.7 %attn_bwd.1 = bf16[32,192,128]{2,1,0:T(8,128)(2,1)S(1)} custom-call(s32[16]{0:T(128)S(1)} %broadcast_select_fusion.hi_ref, bf16[32,192,128]{2,1,0:T(8,128)(2,1)S(1)} %all-to-all-done.r_ref, bf16[32,64,128]{2,1,0:T(8,128)(2,1)S(1)} %all-to-all-done.2.do_ref, f32[32,64,128]{2,1,0:T(8,128)S(1)} %copy-done.4, f32[16,1,256]{2,1,0:T(1,128)S(1)} %get-tuple-element.13.lse_ref), custom_call_target="tpu_custom_call" | custom-call | tf_op jit(solution)/shard_map/attn_bwd/pallas_call | solution.py:129
  207.8 19.9 %all-to-all-start.3 = ((bf16[32,192,128]{2,1,0:T(8,128)(2,1)}), bf16[32,192,128]{2,1,0:T(8,128)(2,1)S(1)}, u32[]{:S(2)}, u32[]{:S(2)}) async-start(bf16[32,192,128]{2,1,0:T(8,128)(2,1)} %copy-done.2), calls=%async_computation.3 | async-start | bytes 3145728 | tf_op jit(solution)/shard_map/all_to_all | solution.py:227
  229.1 2.5 convolution_convert_fusion.2
  231.6 4.5 convolution_convert_fusion.1
  236.2 4.5 convolution_convert_fusion
  240.6 24.9 %all-to-all-done.3 = bf16[32,192,128]{2,1,0:T(8,128)(2,1)S(1)} async-done(((bf16[32,192,128]{2,1,0:T(8,128)(2,1)}), bf16[32,192,128]{2,1,0:T(8,128)(2,1)S(1)}, u32[]{:S(2)}, u32[]{:S(2)}) %all-to-all-start.3) | async-done | bytes 1572896 | tf_op jit(solution)/shard_map/all_to_all | solution.py:227
  269.9 1.5 convolution_convert_fusion.3
  271.5 1.5 convolution_convert_fusion.4
  273.5 1.5 convolution_convert_fusion.5
  275.0 6.3 %fusion.7 = bf16[256,768]{1,0:T(8,128)(2,1)} fusion(f32[256,768]{1,0:T(8,128)S(1)} %copy-done.8, bf16[3072,768]{1,0:T(8,128)(2,1)} %param.19, f32[256,3072]{1,0:T(8,128)} %get-tuple-element.54), kind=kOutput, calls=%fused_computation.22 | convolution fusion | flops 1215430656 | bytes 9043968 | tf_op jit(solution)/shard_map/dot_general | solution.py:158
  284.3 40.6 %all-reduce.2 = (f32[768]{0:T(1024)}, f32[768]{0:T(1024)}) all-reduce(f32[768]{0:T(1024)S(1)} %get-tuple-element.16, f32[768]{0:T(1024)S(1)} %copy-done.48), channel_id=1, replica_groups=mesh['frame'=16,'space'=2] {'frame','space'}, use_global_device_ids=true, to_apply=%region_15.16 | all-reduce | flops 1536 | bytes 12288 | tf_op jit(solution)/shard_map/psum | solution.py:293
  326.2 201.4 %all-reduce.6.cloned.1.call-done = (bf16[768,768]{1,0:T(8,128)(2,1)}, bf16[768,768]{1,0:T(8,128)(2,1)}, bf16[768,768]{1,0:T(8,128)(2,1)}, bf16[768,768]{1,0:T(8,...) async-done(((bf16[768,768]{1,0:T(8,128)(2,1)}, bf16[768,768]{1,0:T(8,128)(2,1)}, bf16[768,768]{1,0:T(8,128)(2,1)}, bf16[768,768]{1,0:T(8,128)(2,1)}, ...) | async-done | bytes 14155792 | tf_op jit(solution)/shard_map/psum | solution.py:290
  527.7 3.0 convert_element_type.185
  530.7 1.6 convert_element_type.187
  532.2 1.6 convert_element_type.189
  533.8 1.6 convert_element_type.191
  536.3 5.0 convert_element_type.193
  541.4 4.5 convert_element_type.195
  (179 shorter events, 39.9 us)
Async XLA Ops:
  7.2 125.6 %copy-start = (bf16[768,768]{1,0:T(8,128)(2,1)S(1)}, bf16[768,768]{1,0:T(8,128)(2,1)}, u32[]{:S(2)}) copy-start(bf16[768,768]{1,0:T(8,128)(2,1)} %param.16) | copy-start | bytes 3538948
  7.2 9.6 %copy-start.12 = (bf16[768,768]{1,0:T(8,128)(2,1)S(1)}, bf16[768,768]{1,0:T(8,128)(2,1)}, u32[]{:S(2)}) copy-start(bf16[768,768]{1,0:T(8,128)(2,1)} %param.14) | copy-start | bytes 3538948
  29.4 8.6 %copy-start.50 = (s32[16]{0:T(128)S(1)}, s32[16]{0:T(128)}, u32[]{:S(2)}) copy-start(s32[16]{0:T(128)} %get-tuple-element.21) | copy-start | bytes 196
  30.8 85.0 %copy-start.17 = (bf16[2,128,768]{2,1,0:T(8,128)(2,1)S(1)}, bf16[2,128,768]{2,1,0:T(8,128)(2,1)}, u32[]{:S(2)}) copy-start(bf16[2,128,768]{2,1,0:T(8,128)(2,1)} %param.21) | copy-start | bytes 1179652
  30.8 45.0 %all-to-all-start = ((bf16[32,192,128]{2,1,0:T(8,128)(2,1)}), bf16[32,192,128]{2,1,0:T(8,128)(2,1)S(1)}, u32[]{:S(2)}, u32[]{:S(2)}) async-start(bf16[32,192,128]{2,1,0:T(8,128)(2,1)} %pad.8), calls=%async_computation | async-start | bytes 3145728 | tf_op jit(solution)/shard_map/all_to_all | solution.py:224
  105.2 25.9 %all-to-all-start.1 = ((bf16[32,64,128]{2,1,0:T(8,128)(2,1)}), bf16[32,64,128]{2,1,0:T(8,128)(2,1)}, u32[]{:S(2)}, u32[]{:S(2)}) async-start(bf16[32,64,128]{2,1,0:T(8,128)(2,1)} %convert_element_type.165), calls=%async_computation.1 | async-start | bytes 1048576 | tf_op jit(solution)/shard_map/all_to_all | solution.py:227
  115.8 17.0 %copy-start.5 = (bf16[2,128,768]{2,1,0:T(8,128)(2,1)S(1)}, bf16[2,128,768]{2,1,0:T(8,128)(2,1)}, u32[]{:S(2)}) copy-start(bf16[2,128,768]{2,1,0:T(8,128)(2,1)} %param.11) | copy-start | bytes 1179652
  133.5 10.3 %copy-start.7 = (f32[256,768]{1,0:T(8,128)}, f32[256,768]{1,0:T(8,128)S(1)}, u32[]{:S(2)}) copy-start(f32[256,768]{1,0:T(8,128)S(1)} %get-tuple-element.52) | copy-start | bytes 2359300
  133.5 10.3 %copy-start.38 = (f32[256]{0:T(256)}, f32[256]{0:T(256)S(1)}, u32[]{:S(2)}) copy-start(f32[256]{0:T(256)S(1)} %broadcast_multiply_fusion.1) | copy-start | bytes 3076
  133.5 7.9 %slice-start.2 = ((s8[4718592]{0:T(1024)(128)(4,1)}), s8[4194304]{0:T(1024)(128)(4,1)S(1)}, s32[]{:S(2)}) async-start(s8[4718592]{0:T(1024)(128)(4,1)} %bitcast.138), calls=%async_computation.7 | async-start | bytes 8388608
  133.8 10.0 %copy-start.44 = (f32[256]{0:T(256)}, f32[256]{0:T(256)S(1)}, u32[]{:S(2)}) copy-start(f32[256]{0:T(256)S(1)} %fusion.31) | copy-start | bytes 3076
  133.8 7.7 %slice-start.3 = ((s8[4718592]{0:T(1024)(128)(4,1)}), s8[524288]{0:T(1024)(128)(4,1)S(1)}, s32[]{:S(2)}) async-start(s8[4718592]{0:T(1024)(128)(4,1)} %bitcast.138), calls=%async_computation.8 | async-start | bytes 1048576
  145.0 5.3 copy-start.21
  146.3 7.1 %copy-start.49 = (s32[16]{0:T(128)S(1)}, s32[16]{0:T(128)}, u32[]{:S(2)}) copy-start(s32[16]{0:T(128)} %get-tuple-element.22) | copy-start | bytes 196
  146.3 22.7 %copy-start.4 = (f32[32,64,128]{2,1,0:T(8,128)S(1)}, f32[32,64,128]{2,1,0:T(8,128)}, u32[]{:S(2)}) copy-start(f32[32,64,128]{2,1,0:T(8,128)} %copy-done.3) | copy-start | bytes 3145732
  150.3 18.6 %all-to-all-start.2 = ((bf16[32,64,128]{2,1,0:T(8,128)(2,1)}), bf16[32,64,128]{2,1,0:T(8,128)(2,1)S(1)}, u32[]{:S(2)}, u32[]{:S(2)}) async-start(bf16[32,64,128]{2,1,0:T(8,128)(2,1)} %pad.9), calls=%async_computation.2 | async-start | bytes 1048576 | tf_op jit(solution)/shard_map/all_to_all | solution.py:224
  169.0 59.1 %copy-start.43 = (f32[2,128]{1,0:T(2,128)S(1)}, f32[2,128]{1,0:T(2,128)}, u32[]{:S(2)}) copy-start(f32[2,128]{1,0:T(2,128)} %copy-done.42) | copy-start | bytes 3076
  169.0 59.1 %copy-start.35 = (f32[768]{0:T(1024)S(1)}, f32[768]{0:T(1024)}, u32[]{:S(2)}) copy-start(f32[768]{0:T(1024)} %param.12) | copy-start | bytes 9220
  207.8 20.3 %copy-start.6 = (bf16[2,128,768]{2,1,0:T(8,128)(2,1)S(1)}, bf16[2,128,768]{2,1,0:T(8,128)(2,1)}, u32[]{:S(2)}) copy-start(bf16[2,128,768]{2,1,0:T(8,128)(2,1)} %param.11) | copy-start | bytes 1179652
  207.8 21.3 %copy-start.20 = (bf16[2,12,1,64,128]{4,0,3,1,2:T(2,128)(2,1)S(1)}, bf16[2,12,1,64,128]{4,0,3,1,2:T(2,128)(2,1)}, u32[]{:S(2)}) copy-start(bf16[2,12,1,64,128]{4,0,3,1,2:T(2,128)(2,1)} %copy-done.19) | copy-start | bytes 1179652
  207.8 23.8 %copy-start.8 = (f32[256,768]{1,0:T(8,128)S(1)}, f32[256,768]{1,0:T(8,128)}, u32[]{:S(2)}) copy-start(f32[256,768]{1,0:T(8,128)} %copy-done.7) | copy-start | bytes 2359300
  207.8 23.8 %copy-start.34 = (f32[768]{0:T(1024)S(1)}, f32[768]{0:T(1024)}, u32[]{:S(2)}) copy-start(f32[768]{0:T(1024)} %param.17) | copy-start | bytes 9220
  207.8 23.8 %copy-start.39 = (f32[256]{0:T(256)S(1)}, f32[256]{0:T(256)}, u32[]{:S(2)}) copy-start(f32[256]{0:T(256)} %copy-done.38) | copy-start | bytes 3076
  207.8 57.7 %all-to-all-start.3 = ((bf16[32,192,128]{2,1,0:T(8,128)(2,1)}), bf16[32,192,128]{2,1,0:T(8,128)(2,1)S(1)}, u32[]{:S(2)}, u32[]{:S(2)}) async-start(bf16[32,192,128]{2,1,0:T(8,128)(2,1)} %copy-done.2), calls=%async_computation.3 | async-start | bytes 3145728 | tf_op jit(solution)/shard_map/all_to_all | solution.py:227
  227.8 299.9 %all-reduce.6.cloned.1.call-start = ((), (), s32[]{:S(2)}) async-start(), calls=%async_computation.4 | async-start | bytes 28311552 | tf_op jit(solution)/shard_map/psum | solution.py:290
  231.6 4.5 copy-start.18
  275.0 6.3 %copy-start.15 = (bf16[768,768]{1,0:T(8,128)(2,1)S(1)}, bf16[768,768]{1,0:T(8,128)(2,1)}, u32[]{:S(2)}) copy-start(bf16[768,768]{1,0:T(8,128)(2,1)} %param.13) | copy-start | bytes 3538948
  283.2 41.7 %copy-start.10 = (f32[256,768]{1,0:T(8,128)S(1)}, f32[256,768]{1,0:T(8,128)}, u32[]{:S(2)}) copy-start(f32[256,768]{1,0:T(8,128)} %copy-done.9) | copy-start | bytes 2359300
  283.2 41.7 %copy-start.47 = (f32[256]{0:T(256)S(1)}, f32[256]{0:T(256)}, u32[]{:S(2)}) copy-start(f32[256]{0:T(256)} %copy-done.46) | copy-start | bytes 3076
  527.7 4.6 copy-start.28
  533.8 7.5 %slice-start = ((s8[4718592]{0:T(1024)(128)(4,1)}), s8[4194304]{0:T(1024)(128)(4,1)S(1)}, s32[]{:S(2)}) async-start(s8[4718592]{0:T(1024)(128)(4,1)} %bitcast.115), calls=%async_computation.5 | async-start | bytes 8388608
  536.3 5.1 slice-start.1
  (29 other events, 65.0 us)
Sparse Core Ops, SparseCore 0:
  275.1 252.4 all-reduce.5

commit v2 on v1

--- a/solution.py
+++ b/solution.py
@@ -170,6 +170,121 @@
     )
 
 
+class Ring:
+    def __init__(self):
+        self.frames = lax.axis_size("frame")
+        self.spaces = lax.axis_size("space")
+        self.planes = self.frames // 4
+        frame = lax.axis_index("frame")
+        self.core = lax.axis_index("space")
+        self.plane = frame // 4
+        self.spot = frame % 4
+        self.bits = (frame % 2, (frame // 2) % 2)
+        self.first_bit = jnp.where(self.core == 0, self.bits[0], self.bits[1])
+        self.second_bit = jnp.where(self.core == 0, self.bits[1], self.bits[0])
+
+    def send(self, value, target):
+        moves = []
+        for frame in range(self.frames):
+            for core in range(self.spaces):
+                to_frame, to_core = target(frame, core)
+                moves.append((frame * self.spaces + core, to_frame * self.spaces + to_core))
+        return lax.ppermute(value, ("frame", "space"), moves)
+
+    def first(self, value):
+        return self.send(value, lambda frame, core: (frame ^ (1 if core == 0 else 2), core))
+
+    def second(self, value):
+        return self.send(value, lambda frame, core: (frame ^ (2 if core == 0 else 1), core))
+
+    def across(self, value):
+        return self.send(value, lambda frame, core: (frame, 1 - core))
+
+    def up(self, value, step):
+        size = self.frames
+        return self.send(value, lambda frame, core: ((frame + 4 * step) % size, core))
+
+    def plane_sum(self, value):
+        count = self.planes
+        rows, columns = value.shape
+        cut = value.reshape(count, rows // count, columns)
+        pick = lambda index: lax.dynamic_index_in_dim(cut, index % count, 0, keepdims=False)
+        total = pick(self.plane)
+        for step in range(1, count):
+            piece = pick(self.plane + step).astype(jnp.bfloat16)
+            total = total + self.up(piece, step).astype(jnp.float32)
+        total = total.astype(jnp.bfloat16)
+        parts = [total] + [self.up(total, step) for step in range(1, count)]
+        twice = jnp.stack(parts[::-1] * 2)
+        start = (count - 1 - self.plane) % count
+        whole = lax.dynamic_slice_in_dim(twice, start, count, 0)
+        return whole.reshape(rows, columns)
+
+    def plane_gather(self, value):
+        one = self.second(value)
+        pair = jnp.stack([value, one])
+        two = self.first(pair)
+        mine = jnp.concatenate([pair, two], axis=0)
+        return mine, self.across(mine)
+
+    def gather_spots(self):
+        near = jnp.where(self.core == 0, 2, 1)
+        own = jnp.stack([self.spot, self.spot ^ near, self.spot ^ (3 - near), self.spot ^ 3])
+        other = jnp.stack([self.spot, self.spot ^ (3 - near), self.spot ^ near, self.spot ^ 3])
+        cores = jnp.repeat(jnp.stack([self.core, 1 - self.core]), 4)
+        return jnp.concatenate([own, other]), cores
+
+    def half_sums(self, value):
+        for bit, exchange in ((self.first_bit, self.first), (self.second_bit, self.second)):
+            rows, columns = value.shape
+            cut = value.reshape(2, rows // 2, columns)
+            keep = lax.dynamic_index_in_dim(cut, bit, 0, keepdims=False)
+            give = lax.dynamic_index_in_dim(cut, 1 - bit, 0, keepdims=False)
+            value = keep + exchange(give.astype(jnp.bfloat16)).astype(jnp.float32)
+        return value
+
+
+def quarter_rows(spots, cores):
+    return jnp.where(cores == 1, spots, (spots % 2) * 2 + spots // 2)
+
+
+def place(mine, other, block_of, out_shape, cuts):
+    count, rows, columns = mine.shape
+    width = columns // cuts
+
+    def body(where, mine_ref, other_ref, *outs):
+        step = pl.program_id(0)
+
+        def put(ref):
+            for index, out in enumerate(outs):
+                out[...] = ref[0, :, index * width : (index + 1) * width].astype(jnp.float32)
+
+        @pl.when(step < count)
+        def _():
+            put(mine_ref)
+
+        @pl.when(step >= count)
+        def _():
+            put(other_ref)
+
+    spec = pl.BlockSpec((rows, width), lambda i, where: (where[0, i], where[1, i]))
+    return pl.pallas_call(
+        body,
+        grid_spec=pltpu.PrefetchScalarGridSpec(
+            num_scalar_prefetch=1,
+            grid=(2 * count,),
+            in_specs=[
+                pl.BlockSpec((1, rows, columns), lambda i, where: (jnp.minimum(i, count - 1), 0, 0)),
+                pl.BlockSpec((1, rows, columns), lambda i, where: (jnp.maximum(i - count, 0), 0, 0)),
+            ],
+            out_specs=[spec] * cuts,
+        ),
+        out_shape=[jax.ShapeDtypeStruct(out_shape, jnp.float32)] * cuts,
+        compiler_params=pltpu.CompilerParams(vmem_limit_bytes=40 * 2**20),
+        name="place",
+    )(block_of, mine, other)
+
+
 def local(
     block_input,
     norm1_gain,
@@ -210,6 +325,22 @@
     angles = frequency[:, None, None] * position[None]
     cosine, sine = jnp.cos(angles), jnp.sin(angles)
 
+    ring = Ring()
+    spots, cores = ring.gather_spots()
+    slots = 4 * spaces
+    hidden_width = w_up.shape[1]
+    part = hidden_width // slots
+    my_part = (ring.spot * spaces + ring.core) * part
+
+    def plane_tokens(value):
+        mine, other = ring.plane_gather(value)
+        return jnp.concatenate([mine, other], axis=0).reshape(slots * tokens, width)
+
+    cot_flat = cotangent.reshape(tokens, width)
+    cot_plane = plane_tokens(cot_flat)
+    up_part = lax.dynamic_slice_in_dim(w_up, my_part, part, 1)
+    down_part = lax.dynamic_slice_in_dim(w_down, my_part, part, 0)
+
     mine = frame_place * spaces + space_place
     my_stream = jnp.minimum(mine // heads, streams - 1)
     idle = mine >= pairs
@@ -230,6 +361,7 @@
 
     input_flat = block_input.astype(jnp.float32).reshape(tokens, width)
     normed = layer_norm(input_flat, norm1_gain).astype(low)
+    normed_pair = jnp.concatenate([normed, ring.across(normed)], axis=0)
 
     def project(weight):
         return dot(weight, normed, 0, 1)
@@ -246,15 +378,18 @@
     attended_own, lse = attn_fwd(lo, packed, frames)
     attended = to_tokens(attended_own.astype(low), 1)[0].reshape(width, tokens)
 
+    attended_other = ring.across(attended)
     middle = input_flat + dot(attended, w_out, 0, 0)
     normed_two = layer_norm(middle, norm2_gain).astype(low)
-    hidden = dot(normed_two, w_up, 1, 0)
-    activated, gelu_back = jax.vjp(lambda inner: jax.nn.gelu(inner, approximate=True), hidden)
-    activated_low = activated.astype(low)
-    block_output = (middle + dot(activated_low, w_down, 1, 0)).astype(low)
-    cot_flat = cotangent.reshape(tokens, width)
-    d_activated = dot(cot_flat, w_down, 1, 1)
-    d_hidden = gelu_back(d_activated)[0].astype(low)
+    two_plane = plane_tokens(normed_two)
+    gelu = lambda inner: jax.nn.gelu(inner, approximate=True)
+
+    def feed(rows_two, rows_cot, up_weight, down_weight):
+        activated, gelu_back = jax.vjp(gelu, dot(rows_two, up_weight, 1, 0))
+        d_hidden = gelu_back(dot(rows_cot, down_weight, 1, 1))[0].astype(low)
+        return activated.astype(low), d_hidden
+
+    activated_low, d_hidden = feed(normed_two, cot_flat, w_up, w_down)
     d_normed_two = dot(d_hidden, w_up, 1, 1)
     unused_two, norm_two_back = jax.vjp(layer_norm, middle, norm2_gain)
     d_middle_norm, grad_gain_two = norm_two_back(d_normed_two)
@@ -262,11 +397,31 @@
     d_branch = d_middle.astype(low)
     d_attended = dot(w_out, d_branch, 1, 1).astype(low)
     d_own = to_heads([d_attended.reshape(heads, head_width, streams, rows)])
-
-    grad_down = dot(activated_low, cot_flat, 0, 0)
-    grad_up = dot(normed_two, d_hidden, 0, 0)
-    grad_out = dot(attended, d_branch, 1, 0)
-    early = lax.psum((grad_down.astype(low), grad_up.astype(low), grad_out.astype(low)), axes)
+    block_output = (middle + dot(activated_low, w_down, 1, 0)).astype(low)
+
+    part_active, part_hidden = feed(two_plane, cot_plane, up_part, down_part)
+    grad_up = ring.plane_sum(dot(two_plane, part_hidden, 0, 0))
+    grad_down = ring.plane_sum(dot(part_active, cot_plane, 0, 0))
+    parts_of = spots * spaces + cores
+    zeros = jnp.zeros_like(parts_of)
+    (grad_up,) = place(
+        *ring.plane_gather(grad_up), jnp.stack([zeros, parts_of]), w_up.shape, 1
+    )
+    (grad_down,) = place(
+        *ring.plane_gather(grad_down), jnp.stack([parts_of, zeros]), w_down.shape, 1
+    )
+    quarters = jnp.stack([quarter_rows(spots, cores), cores])
+    half_columns = width // spaces
+
+    def my_half(value, axis, core):
+        return lax.dynamic_slice_in_dim(value, core * half_columns, half_columns, axis)
+
+    branch_other = ring.across(my_half(d_branch, 1, 1 - ring.core))
+    grad_out = dot(attended, my_half(d_branch, 1, ring.core), 1, 0) + dot(
+        attended_other, branch_other, 1, 0
+    )
+    grad_out = ring.plane_sum(ring.half_sums(grad_out))
+    (grad_out,) = place(*ring.plane_gather(grad_out), quarters, w_out.shape, 1)
 
     grads_own = attn_bwd(hi, packed, d_own, attended_own, lse, frames)
     d_three = to_tokens(grads_own, 3)
@@ -278,31 +433,32 @@
     d_query = (rope_back(d_three[0]) * scale).astype(low)
     d_key = rope_back(d_three[1]).astype(low)
     d_value = d_three[2].reshape(width, tokens)
-    grad_query = dot(normed, d_query, 0, 1)
-    grad_key = dot(normed, d_key, 0, 1)
-    grad_value = dot(normed, d_value, 0, 1)
+    d_three = jnp.stack([d_query, d_key, d_value])
+    three_other = ring.across(my_half(d_three, 1, 1 - ring.core))
+    three_pair = jnp.concatenate([my_half(d_three, 1, ring.core), three_other], axis=2)
+    grad_three = dot(normed_pair, three_pair.reshape(3 * half_columns, spaces * tokens), 0, 1)
+    grad_three = ring.plane_sum(ring.half_sums(grad_three))
+    grad_query, grad_key, grad_value = place(
+        *ring.plane_gather(grad_three), quarters, w_query.shape, 3
+    )
     d_normed = (
         dot(d_query, w_query, 0, 1) + dot(d_key, w_key, 0, 1) + dot(d_value, w_value, 0, 1)
     )
     unused_one, norm_one_back = jax.vjp(layer_norm, input_flat, norm1_gain)
     d_input_norm, grad_gain_one = norm_one_back(d_normed)
     grad_input = (d_middle + d_input_norm).reshape(streams, rows, width)
-    late = lax.psum(
-        (grad_query.astype(low), grad_key.astype(low), grad_value.astype(low)), axes
-    )
-    gains = lax.psum((grad_gain_one, grad_gain_two), axes)
-    wide = lambda member: member.astype(jnp.float32)
+    gain_sum = lambda value: jnp.sum(lax.all_gather(value, axes), axis=0)
     return (
         block_output.reshape(streams, rows, width),
         grad_input,
-        gains[0],
-        wide(late[0]),
-        wide(late[1]),
-        wide(late[2]),
-        wide(early[2]),
-        gains[1],
-        wide(early[1]),
-        wide(early[0]),
+        gain_sum(grad_gain_one),
+        grad_query,
+        grad_key,
+        grad_value,
+        grad_out,
+        gain_sum(grad_gain_two),
+        grad_up,
+        grad_down,
     )
 
 

time: 554 us -> 564 us (1.018); the launches traced: 553 us -> 554 us
  waiting for transfers between devices: 289 us -> 127 us
  starting transfers between devices: 41.1 us -> 113 us
  blocking collectives: 40.6 us -> 77.8 us
  Pallas kernels: 65.3 us -> 93.1 us
  local copies, waits for them, and re-layouts: 20.4 us -> 43.7 us
  other arithmetic: 35.1 us -> 52.2 us
  between operations: 14.9 us -> 2.47 us
    psum x1 -> x0, waiting for transfers between devices: 201 us -> none  [local(): lax.psum((grad_query.astype(low), grad_key.astype(low), grad_value.astype...]
    ppermute x0 -> x50, waiting for transfers between devices: none -> 89.3 us  [send(): return lax.ppermute(value, ('frame', 'space'), moves)]
    all_gather x0 -> x2, blocking collectives: none -> 77.8 us  [local(): gain_sum = lambda value: jnp.sum(lax.all_gather(value, axes), axis=0)]
    ppermute x0 -> x50, starting transfers between devices: none -> 72.5 us  [send(): return lax.ppermute(value, ('frame', 'space'), moves)]
    psum x1 -> x0, blocking collectives: 40.6 us -> none  [local(): gains = lax.psum((grad_gain_one, grad_gain_two), axes)]
    all_to_all x2, waiting for transfers between devices: 34.8 us -> 0.16 us  [to_tokens(): back = lax.all_to_all(whole, axes, 0, 0, tiled=True)[:pairs]]
    pallas_call x0 -> x4, Pallas kernels: none -> 27.8 us  [place(): pl.pallas_call(body, grid_spec=pltpu.PrefetchScalarGridSpec(num_scalar_pr...]
    concatenate x0 -> x9, other arithmetic: none -> 17.5 us  [the longest x6 11.2 us: plane_gather(): mine = jnp.concatenate([pair, two], axis=0)]
  transfers between devices with their start and end apart: 5 -> 54, of which waited for: 5 -> 18; matrix products, arithmetic and copies ran while one was open for 5% -> 20% of each run, Pallas kernels for 0% -> 10%
where the time goes in v2:
time: 564 us; the launch traced here: 554 us
  waiting for transfers between devices  127 us (23%)
  starting transfers between devices  113 us (20%)
  Pallas kernels  93.1 us (17%)
  blocking collectives  77.8 us (14%)
  other arithmetic  52.2 us (9%)
  matrix products  45.4 us (8%)
  local copies, waits for them, and re-layouts  43.7 us (8%)
    ppermute x50, waiting for transfers between devices, send(): return lax.ppermute(value, ('frame', 'space'), moves)  89.3 us
    all_gather x2, blocking collectives, local(): gain_sum = lambda value: jnp.sum(lax.all_gather(value, axes), axis=0)  77.8 us
    ppermute x50, starting transfers between devices, send(): return lax.ppermute(value, ('frame', 'space'), moves)  72.5 us
    dot_general x17, matrix products, dot(): lax.dot_general(left, right, (((left_dim,), (right_dim,)), ((), ())), pre...  45.4 us
    all_to_all x2, waiting for transfers between devices, to_heads(): return lax.all_to_all(whole, axes, 0, 0, tiled=True)  37.7 us
    pallas_call x1, Pallas kernels, attn_bwd(): pl.pallas_call(functools.partial(bwd_kernel, nf=nf, rows=rows), out_shape...  37.7 us
    all_to_all x2, starting transfers between devices, to_tokens(): back = lax.all_to_all(whole, axes, 0, 0, tiled=True)[:pairs]  30.1 us
    pallas_call x4, Pallas kernels, place(): pl.pallas_call(body, grid_spec=pltpu.PrefetchScalarGridSpec(num_scalar_pr...  27.8 us
  transfers between devices with their start and end apart: 54, of which 18 were waited for; matrix products, arithmetic and copies ran while one was open for 20% of the time, Pallas kernels for 10%

profile of v2, /device:TPU:0, one launch (start us, length us, event | category | flops | bytes accessed | tf_op | source)
XLA Modules:
  0.0 554.4 jit_solution(5567020336363746713)
XLA Ops:
  24.6 7.3 %all-to-all-start = ((bf16[32,192,128]{2,1,0:T(8,128)(2,1)}), bf16[32,192,128]{2,1,0:T(8,128)(2,1)S(1)}, u32[]{:S(2)}, u32[]{:S(2)}) async-start(bf16[32,192,128]{2,1,0:T(8,128)(2,1)} %pad.10), calls=%async_computation | async-start | bytes 3145728 | tf_op jit(solution)/shard_map/all_to_all | solution.py:355
  31.9 37.7 %all-to-all-done.r_ref = bf16[32,192,128]{2,1,0:T(8,128)(2,1)S(1)} async-done(((bf16[32,192,128]{2,1,0:T(8,128)(2,1)}), bf16[32,192,128]{2,1,0:T(8,128)(2,1)S(1)}, u32[]{:S(2)}, u32[]{:S(2)}) %all-to-all-start) | async-done | bytes 1572896 | tf_op jit(solution)/shard_map/all_to_all | solution.py:355
  69.6 27.6 %attn_fwd.1 = (f32[32,64,128]{2,1,0:T(8,128)S(1)}, f32[16,1,256]{2,1,0:T(1,128)S(1)}) custom-call(s32[16]{0:T(128)S(1)} %broadcast_select_fusion.1.lo_ref, bf16[32,192,128]{2,1,0:T(8,128)(2,1)S(1)} %all-to-all-done.r_ref), custom_call_target="tpu_custom_call" | custom-call | tf_op jit(solution)/shard_map/attn_fwd/pallas_call | solution.py:69
  99.1 10.8 %all-to-all-start.1 = ((bf16[32,64,128]{2,1,0:T(8,128)(2,1)}), bf16[32,64,128]{2,1,0:T(8,128)(2,1)}, u32[]{:S(2)}, u32[]{:S(2)}) async-start(bf16[32,64,128]{2,1,0:T(8,128)(2,1)} %convert_element_type.291), calls=%async_computation.1 | async-start | bytes 1048576 | tf_op jit(solution)/shard_map/all_to_all | solution.py:358
  112.2 9.4 %collective-permute-done.29 = bf16[256,768]{1,0:T(8,128)(2,1)} collective-permute-done((bf16[256,768]{1,0:T(8,128)(2,1)S(1)}, bf16[256,768]{1,0:T(8,128)(2,1)}, u32[]{:S(2)}, u32[]{:S(2)}) %collective-permute-start.29) | collective-permute-done | bytes 393248 | tf_op jit(solution)/shard_map/ppermute | solution.py:192
  130.2 5.5 fusion.116
  135.7 9.4 %multiply_reduce_fusion = (f32[768]{0:T(1024)S(1)}, f32[256]{0:T(256)S(1)}, f32[256,768]{1,0:T(8,128)}) fusion(f32[256,768]{1,0:T(8,128)} %copy-done.5, f32[256]{0:T(256)S(1)} %fusion.89, f32[256]{0:T(256)S(1)} %broadcast_multiply_fusion.1, f32[768]{0:T(1024)S(1)} %copy-done.56, bf16[768,3072]{1,0:T(8,128)(2,1)} %param.18, f32[256,3072]{1,0:T(8,128)} %fusion.116, ...), kind=kOutput, calls=%fused_computation.77 | convolution fusion | flops 2433022976 | bytes 14558208 | tf_op jit(solution)/shard_map/dot_general | solution.py:158
  162.9 6.0 %collective-permute-done.16 = bf16[192,384]{1,0:T(8,128)(2,1)S(1)} collective-permute-done((bf16[192,384]{1,0:T(8,128)(2,1)S(1)}, bf16[192,384]{1,0:T(8,128)(2,1)S(1)}, u32[]{:S(2)}, u32[]{:S(2)}) %collective-permute-start.16) | collective-permute-done | bytes 147488 | tf_op jit(solution)/shard_map/ppermute | solution.py:192
  189.8 13.1 %collective-permute-done.21 = bf16[48,384]{1,0:T(8,128)(2,1)S(1)} collective-permute-done((bf16[48,384]{1,0:T(8,128)(2,1)S(1)}, bf16[48,384]{1,0:T(8,128)(2,1)S(1)}, u32[]{:S(2)}, u32[]{:S(2)}) %collective-permute-start.21) | collective-permute-done | bytes 36896 | tf_op jit(solution)/shard_map/ppermute | solution.py:192
  210.2 37.7 %attn_bwd.1 = bf16[32,192,128]{2,1,0:T(8,128)(2,1)S(1)} custom-call(s32[16]{0:T(128)S(1)} %broadcast_select_fusion.hi_ref, bf16[32,192,128]{2,1,0:T(8,128)(2,1)S(1)} %all-to-all-done.r_ref, bf16[32,64,128]{2,1,0:T(8,128)(2,1)S(1)} %all-to-all-done.2.do_ref, f32[32,64,128]{2,1,0:T(8,128)S(1)} %copy-done.4, f32[16,1,256]{2,1,0:T(1,128)S(1)} %get-tuple-element.16.lse_ref), custom_call_target="tpu_custom_call" | custom-call | tf_op jit(solution)/shard_map/attn_bwd/pallas_call | solution.py:129
  249.1 19.3 %all-to-all-start.3 = ((bf16[32,192,128]{2,1,0:T(8,128)(2,1)}), bf16[32,192,128]{2,1,0:T(8,128)(2,1)S(1)}, u32[]{:S(2)}, u32[]{:S(2)}) async-start(bf16[32,192,128]{2,1,0:T(8,128)(2,1)} %copy-done.2), calls=%async_computation.3 | async-start | bytes 3145728 | tf_op jit(solution)/shard_map/all_to_all | solution.py:358
  274.9 4.7 copy.77
  279.6 6.0 %fusion.21 = (bf16[384,2048]{1,0:T(8,128)(2,1)S(1)}, f32[2048,384]{0,1:T(8,128)}) fusion(bf16[2048,768]{1,0:T(8,128)(2,1)} %bitcast.276, bf16[768,3072]{1,0:T(8,128)(2,1)} %param.18, s32[]{:T(128)S(6)} %select_n.252), kind=kOutput, calls=%fused_computation.26 | convolution fusion | flops 1215037440 | bytes 8454148 | tf_op jit(solution)/shard_map/dot_general | solution.py:158
  292.3 3.5 copy.81
  295.8 8.2 %fusion.23 = f32[4,192,384]{2,1,0:T(8,128)S(1)} fusion(bf16[4,192,2048]{2,1,0:T(8,128)(2,1)} %bitcast.310, f32[2048,384]{1,0:T(8,128)} %copy.81, bf16[2048,768]{1,0:T(8,128)(2,1)} %bitcast.308, bf16[3072,768]{1,0:T(8,128)(2,1)} %param.19, s32[]{:T(128)S(6)} %select_n.252), kind=kOutput, calls=%fused_computation.38 | convolution fusion | flops 2431647744 | bytes 11206660 | tf_op jit(solution)/shard_map/dot_general | solution.py:158
  308.0 11.6 %collective-permute-start.33 = (bf16[192,384]{1,0:T(8,128)(2,1)S(1)}, bf16[192,384]{1,0:T(8,128)(2,1)S(1)}, u32[]{:S(2)}, u32[]{:S(2)}) collective-permute-start(bf16[192,384]{1,0:T(8,128)(2,1)S(1)} %get-tuple-element.36), channel_id=1, source_target_pairs={{0,16},{1,17},{2,18},{3,19},{4,20},{5,21},{6,22},{7,23},{8,24},{9,... | collective-permute-start | bytes 442376 | tf_op jit(solution)/shard_map/ppermute | solution.py:192
  323.8 5.2 collective-permute-start.45
  329.4 8.9 %collective-permute-done.33 = bf16[192,384]{1,0:T(8,128)(2,1)S(1)} collective-permute-done((bf16[192,384]{1,0:T(8,128)(2,1)S(1)}, bf16[192,384]{1,0:T(8,128)(2,1)S(1)}, u32[]{:S(2)}, u32[]{:S(2)}) %collective-permute-start.33) | collective-permute-done | bytes 147488 | tf_op jit(solution)/shard_map/ppermute | solution.py:192
  342.5 4.3 collective-permute-start.36
  347.5 3.6 collective-permute-start.35
  371.1 10.7 %collective-permute-done.2 = bf16[384,1152]{1,0:T(8,128)(2,1)S(1)} collective-permute-done((bf16[384,1152]{1,0:T(8,128)(2,1)S(1)}, bf16[384,1152]{1,0:T(8,128)(2,1)S(1)}, u32[]{:S(2)}, u32[]{:S(2)}) %collective-permute-start.2) | collective-permute-done | bytes 884768 | tf_op jit(solution)/shard_map/ppermute | solution.py:192
  384.4 6.1 %collective-permute-done.3 = bf16[192,1152]{1,0:T(8,128)(2,1)S(1)} collective-permute-done((bf16[192,1152]{1,0:T(8,128)(2,1)S(1)}, bf16[192,1152]{1,0:T(8,128)(2,1)S(1)}, u32[]{:S(2)}, u32[]{:S(2)}) %collective-permute-start.3) | collective-permute-done | bytes 442400 | tf_op jit(solution)/shard_map/ppermute | solution.py:192
  390.7 3.8 collective-permute-start.6
  394.6 3.9 collective-permute-done.4
  407.8 8.2 %collective-permute-done.8 = bf16[48,1152]{1,0:T(8,128)(2,1)S(1)} collective-permute-done((bf16[48,1152]{1,0:T(8,128)(2,1)S(1)}, bf16[48,1152]{1,0:T(8,128)(2,1)S(1)}, u32[]{:S(2)}, u32[]{:S(2)}) %collective-permute-start.8) | collective-permute-done | bytes 110624 | tf_op jit(solution)/shard_map/ppermute | solution.py:192
  419.5 8.7 %collective-permute-done.10 = bf16[192,1152]{1,0:T(8,128)(2,1)S(1)} collective-permute-done((bf16[192,1152]{1,0:T(8,128)(2,1)S(1)}, bf16[192,1152]{1,0:T(8,128)(2,1)S(1)}, u32[]{:S(2)}, u32[]{:S(2)}) %collective-permute-start.10) | collective-permute-done | bytes 442400 | tf_op jit(solution)/shard_map/ppermute | solution.py:192
  436.5 40.4 %all-gather.3 = f32[32,1,768]{2,1,0:T(1,128)} all-gather(f32[1,1,768]{2,1,0:T(1,128)S(1)} %reshape.1147), channel_id=3, replica_groups=mesh['frame'=16,'space'=2] {'frame','space'}, dimensions={0}, use_global_device_ids=true | all-gather | bytes 101376 | tf_op jit(solution)/shard_map/all_gather | solution.py:450
  478.5 3.6 place.5
  489.3 37.3 %all-gather.2 = f32[32,1,768]{2,1,0:T(1,128)S(1)} all-gather(f32[1,1,768]{2,1,0:T(1,128)S(1)} %reshape.1145), channel_id=2, replica_groups=mesh['frame'=16,'space'=2] {'frame','space'}, dimensions={0}, use_global_device_ids=true | all-gather | bytes 101376 | tf_op jit(solution)/shard_map/all_gather | solution.py:450
  530.0 8.6 %place.6 = f32[768,3072]{1,0:T(8,128)} custom-call(s32[2,8]{1,0:T(2,128)S(1)} %get-tuple-element.66.where, bf16[4,768,384]{2,1,0:T(8,128)(2,1)} %pad_maximum_fusion.2.mine_ref, bf16[4,768,384]{2,1,0:T(8,128)(2,1)} %collective-permute-done.40.other_ref), custom_call_target="tpu_custom_call" | custom-call | tf_op jit(solution)/shard_map/place/pallas_call | solution.py:271
  538.6 7.8 %place.7 = f32[3072,768]{1,0:T(8,128)} custom-call(s32[2,8]{1,0:T(2,128)S(1)} %get-tuple-element.65.where, bf16[4,384,768]{2,1,0:T(8,128)(2,1)S(1)} %pad_maximum_fusion.3.mine_ref, bf16[4,384,768]{2,1,0:T(8,128)(2,1)} %collective-permute-done.49.other_ref), custom_call_target="tpu_custom_call" | custom-call | tf_op jit(solution)/shard_map/place/pallas_call | solution.py:271
  546.4 7.7 %place.4 = (f32[768,768]{1,0:T(8,128)}, f32[768,768]{1,0:T(8,128)}, f32[768,768]{1,0:T(8,128)}) custom-call(s32[2,8]{1,0:T(2,128)S(1)} %pad_add_fusion.where, bf16[4,192,1152]{2,1,0:T(8,128)(2,1)} %pad_maximum_fusion.4.mine_ref, bf16[4,192,1152]{2,1,0:T(8,128)(2,1)} %collective-permute-done.12.other_ref), custom_call_target="tpu_custom_call" | custom-call | tf_op jit(solution)/shard_map/place/pallas_call | solution.py:271
  (388 shorter events, 165.2 us)
Async XLA Ops:
  24.6 45.0 %all-to-all-start = ((bf16[32,192,128]{2,1,0:T(8,128)(2,1)}), bf16[32,192,128]{2,1,0:T(8,128)(2,1)S(1)}, u32[]{:S(2)}, u32[]{:S(2)}) async-start(bf16[32,192,128]{2,1,0:T(8,128)(2,1)} %pad.10), calls=%async_computation | async-start | bytes 3145728 | tf_op jit(solution)/shard_map/all_to_all | solution.py:355
  99.1 26.4 %all-to-all-start.1 = ((bf16[32,64,128]{2,1,0:T(8,128)(2,1)}), bf16[32,64,128]{2,1,0:T(8,128)(2,1)}, u32[]{:S(2)}, u32[]{:S(2)}) async-start(bf16[32,64,128]{2,1,0:T(8,128)(2,1)} %convert_element_type.291), calls=%async_computation.1 | async-start | bytes 1048576 | tf_op jit(solution)/shard_map/all_to_all | solution.py:358
  111.9 40.4 %collective-permute-start = (bf16[256,768]{1,0:T(8,128)(2,1)}, bf16[256,768]{1,0:T(8,128)(2,1)}, u32[]{:S(2)}, u32[]{:S(2)}) collective-permute-start(bf16[256,768]{1,0:T(8,128)(2,1)} %multiply_convert_fusion.7), channel_id=1, source_target_pairs={{0,1},{1,0},{2,3},{3,2},{4,5},{5,4},{6,7},{7,6},{8,9},{9,8},{10,11... | collective-permute-start | bytes 1179656 | tf_op jit(solution)/shard_map/ppermute | solution.py:192
  123.8 32.9 %collective-permute-start.30 = (bf16[2,256,768]{2,1,0:T(8,128)(2,1)}, bf16[2,256,768]{2,1,0:T(8,128)(2,1)}, u32[]{:S(2)}, u32[]{:S(2)}) collective-permute-start(bf16[2,256,768]{2,1,0:T(8,128)(2,1)} %pad_maximum_fusion.12), channel_id=1, source_target_pairs={{0,2},{1,5},{2,0},{3,7},{4,6},{5,1},{6,4},{7,3},{8,10},{9,13},{10,... | collective-permute-start | bytes 2359304 | tf_op jit(solution)/shard_map/ppermute | solution.py:192
  127.8 21.0 %collective-permute-start.13 = (bf16[768,256]{1,0:T(8,128)(2,1)}, bf16[768,256]{1,0:T(8,128)(2,1)}, u32[]{:S(2)}, u32[]{:S(2)}) collective-permute-start(bf16[768,256]{1,0:T(8,128)(2,1)} %bitcast.273), channel_id=1, source_target_pairs={{0,1},{1,0},{2,3},{3,2},{4,5},{5,4},{6,7},{7,6},{8,9},{9,8},{10,11... | collective-permute-start | bytes 1179656 | tf_op jit(solution)/shard_map/ppermute | solution.py:192
  159.4 47.8 %collective-permute-start.31 = (bf16[4,256,768]{2,1,0:T(8,128)(2,1)}, bf16[4,256,768]{2,1,0:T(8,128)(2,1)}, u32[]{:S(2)}, u32[]{:S(2)}) collective-permute-start(bf16[4,256,768]{2,1,0:T(8,128)(2,1)} %pad_maximum_fusion.6), channel_id=1, source_target_pairs={{0,1},{1,0},{2,3},{3,2},{4,5},{5,4},{6,7},{7,6},{8,9},{9,8},{10,11... | collective-permute-start | bytes 4718600 | tf_op jit(solution)/shard_map/ppermute | solution.py:192
  174.8 28.1 %collective-permute-start.27 = (bf16[2,256,768]{2,1,0:T(8,128)(2,1)}, bf16[2,256,768]{2,1,0:T(8,128)(2,1)}, u32[]{:S(2)}, u32[]{:S(2)}) collective-permute-start(bf16[2,256,768]{2,1,0:T(8,128)(2,1)} %pad_maximum_fusion.11), channel_id=1, source_target_pairs={{0,2},{1,5},{2,0},{3,7},{4,6},{5,1},{6,4},{7,3},{8,10},{9,13},{10,... | collective-permute-start | bytes 2359304 | tf_op jit(solution)/shard_map/ppermute | solution.py:192
  182.9 27.3 %all-to-all-start.2 = ((bf16[32,64,128]{2,1,0:T(8,128)(2,1)}), bf16[32,64,128]{2,1,0:T(8,128)(2,1)S(1)}, u32[]{:S(2)}, u32[]{:S(2)}) async-start(bf16[32,64,128]{2,1,0:T(8,128)(2,1)} %pad.11), calls=%async_computation.2 | async-start | bytes 1048576 | tf_op jit(solution)/shard_map/all_to_all | solution.py:355
  185.5 17.4 %collective-permute-start.22 = (bf16[48,384]{1,0:T(8,128)(2,1)S(1)}, bf16[48,384]{1,0:T(8,128)(2,1)S(1)}, u32[]{:S(2)}, u32[]{:S(2)}) collective-permute-start(bf16[48,384]{1,0:T(8,128)(2,1)S(1)} %fusion.80), channel_id=1, source_target_pairs={{0,8},{1,9},{2,10},{3,11},{4,12},{5,13},{6,14},{7,15},{8,16},{9,17... | collective-permute-start | bytes 110600 | tf_op jit(solution)/shard_map/ppermute | solution.py:192
  205.4 66.4 %collective-permute-start.28 = (bf16[4,256,768]{2,1,0:T(8,128)(2,1)}, bf16[4,256,768]{2,1,0:T(8,128)(2,1)}, u32[]{:S(2)}, u32[]{:S(2)}) collective-permute-start(bf16[4,256,768]{2,1,0:T(8,128)(2,1)} %pad_maximum_fusion.5), channel_id=1, source_target_pairs={{0,1},{1,0},{2,3},{3,2},{4,5},{5,4},{6,7},{7,6},{8,9},{9,8},{10,11... | collective-permute-start | bytes 4718600 | tf_op jit(solution)/shard_map/ppermute | solution.py:192
  205.6 62.8 %collective-permute-start.23 = (bf16[192,384]{1,0:T(8,128)(2,1)S(1)}, bf16[192,384]{1,0:T(8,128)(2,1)}, u32[]{:S(2)}, u32[]{:S(2)}) collective-permute-start(bf16[192,384]{1,0:T(8,128)(2,1)S(1)} %bitcast.329), channel_id=1, source_target_pairs={{0,4},{1,3},{2,6},{3,1},{4,0},{5,7},{6,2},{7,5},{8,12},{9,11},{10,... | collective-permute-start | bytes 442376 | tf_op jit(solution)/shard_map/ppermute | solution.py:192
  249.1 106.7 %all-to-all-start.3 = ((bf16[32,192,128]{2,1,0:T(8,128)(2,1)}), bf16[32,192,128]{2,1,0:T(8,128)(2,1)S(1)}, u32[]{:S(2)}, u32[]{:S(2)}) async-start(bf16[32,192,128]{2,1,0:T(8,128)(2,1)} %copy-done.2), calls=%async_computation.3 | async-start | bytes 3145728 | tf_op jit(solution)/shard_map/all_to_all | solution.py:358
  270.0 147.1 %collective-permute-start.24 = (bf16[2,192,384]{2,1,0:T(8,128)(2,1)}, bf16[2,192,384]{2,1,0:T(8,128)(2,1)}, u32[]{:S(2)}, u32[]{:S(2)}) collective-permute-start(bf16[2,192,384]{2,1,0:T(8,128)(2,1)} %pad_maximum_fusion.15), channel_id=1, source_target_pairs={{0,2},{1,5},{2,0},{3,7},{4,6},{5,1},{6,4},{7,3},{8,10},{9,13},{10,... | collective-permute-start | bytes 884744 | tf_op jit(solution)/shard_map/ppermute | solution.py:192
  287.9 17.8 %collective-permute-start.41 = (bf16[96,768]{1,0:T(8,128)(2,1)}, bf16[96,768]{1,0:T(8,128)(2,1)S(1)}, u32[]{:S(2)}, u32[]{:S(2)}) collective-permute-start(bf16[96,768]{1,0:T(8,128)(2,1)} %get-tuple-element.31), channel_id=1, source_target_pairs={{0,8},{1,9},{2,10},{3,11},{4,12},{5,13},{6,14},{7,15},{8,16},{9,17... | collective-permute-start | bytes 442376 | tf_op jit(solution)/shard_map/ppermute | solution.py:192
  289.4 18.6 %collective-permute-start.43 = (bf16[96,768]{1,0:T(8,128)(2,1)}, bf16[96,768]{1,0:T(8,128)(2,1)S(1)}, u32[]{:S(2)}, u32[]{:S(2)}) collective-permute-start(bf16[96,768]{1,0:T(8,128)(2,1)} %get-tuple-element.32), channel_id=1, source_target_pairs={{0,24},{1,25},{2,26},{3,27},{4,28},{5,29},{6,30},{7,31},{8,0},{9,1... | collective-permute-start | bytes 442376 | tf_op jit(solution)/shard_map/ppermute | solution.py:192
  291.7 30.8 %collective-permute-start.42 = (bf16[96,768]{1,0:T(8,128)(2,1)}, bf16[96,768]{1,0:T(8,128)(2,1)}, u32[]{:S(2)}, u32[]{:S(2)}) collective-permute-start(bf16[96,768]{1,0:T(8,128)(2,1)} %get-tuple-element.33), channel_id=1, source_target_pairs={{0,16},{1,17},{2,18},{3,19},{4,20},{5,21},{6,22},{7,23},{8,24},{9,... | collective-permute-start | bytes 442376 | tf_op jit(solution)/shard_map/ppermute | solution.py:192
  304.1 19.7 %collective-permute-start.32 = (bf16[192,384]{1,0:T(8,128)(2,1)S(1)}, bf16[192,384]{1,0:T(8,128)(2,1)S(1)}, u32[]{:S(2)}, u32[]{:S(2)}) collective-permute-start(bf16[192,384]{1,0:T(8,128)(2,1)S(1)} %get-tuple-element.34), channel_id=1, source_target_pairs={{0,8},{1,9},{2,10},{3,11},{4,12},{5,13},{6,14},{7,15},{8,16},{9,17... | collective-permute-start | bytes 442376 | tf_op jit(solution)/shard_map/ppermute | solution.py:192
  305.7 23.3 %collective-permute-start.34 = (bf16[192,384]{1,0:T(8,128)(2,1)S(1)}, bf16[192,384]{1,0:T(8,128)(2,1)S(1)}, u32[]{:S(2)}, u32[]{:S(2)}) collective-permute-start(bf16[192,384]{1,0:T(8,128)(2,1)S(1)} %get-tuple-element.35), channel_id=1, source_target_pairs={{0,24},{1,25},{2,26},{3,27},{4,28},{5,29},{6,30},{7,31},{8,0},{9,1... | collective-permute-start | bytes 442376 | tf_op jit(solution)/shard_map/ppermute | solution.py:192
  308.0 30.4 %collective-permute-start.33 = (bf16[192,384]{1,0:T(8,128)(2,1)S(1)}, bf16[192,384]{1,0:T(8,128)(2,1)S(1)}, u32[]{:S(2)}, u32[]{:S(2)}) collective-permute-start(bf16[192,384]{1,0:T(8,128)(2,1)S(1)} %get-tuple-element.36), channel_id=1, source_target_pairs={{0,16},{1,17},{2,18},{3,19},{4,20},{5,21},{6,22},{7,23},{8,24},{9,... | collective-permute-start | bytes 442376 | tf_op jit(solution)/shard_map/ppermute | solution.py:192
  323.7 28.1 %collective-permute-start.46 = (bf16[96,768]{1,0:T(8,128)(2,1)S(1)}, bf16[96,768]{1,0:T(8,128)(2,1)S(1)}, u32[]{:S(2)}, u32[]{:S(2)}) collective-permute-start(bf16[96,768]{1,0:T(8,128)(2,1)S(1)} %fusion.59), channel_id=1, source_target_pairs={{0,8},{1,9},{2,10},{3,11},{4,12},{5,13},{6,14},{7,15},{8,16},{9,17... | collective-permute-start | bytes 442376 | tf_op jit(solution)/shard_map/ppermute | solution.py:192
  323.8 23.7 %collective-permute-start.45 = (bf16[96,768]{1,0:T(8,128)(2,1)S(1)}, bf16[96,768]{1,0:T(8,128)(2,1)S(1)}, u32[]{:S(2)}, u32[]{:S(2)}) collective-permute-start(bf16[96,768]{1,0:T(8,128)(2,1)S(1)} %fusion.59), channel_id=1, source_target_pairs={{0,16},{1,17},{2,18},{3,19},{4,20},{5,21},{6,22},{7,23},{8,24},{9,... | collective-permute-start | bytes 442376 | tf_op jit(solution)/shard_map/ppermute | solution.py:192
  339.4 29.8 %collective-permute-start.37 = (bf16[192,384]{1,0:T(8,128)(2,1)S(1)}, bf16[192,384]{1,0:T(8,128)(2,1)S(1)}, u32[]{:S(2)}, u32[]{:S(2)}) collective-permute-start(bf16[192,384]{1,0:T(8,128)(2,1)S(1)} %fusion.62), channel_id=1, source_target_pairs={{0,8},{1,9},{2,10},{3,11},{4,12},{5,13},{6,14},{7,15},{8,16},{9,17... | collective-permute-start | bytes 442376 | tf_op jit(solution)/shard_map/ppermute | solution.py:192
  342.5 22.6 %collective-permute-start.36 = (bf16[192,384]{1,0:T(8,128)(2,1)S(1)}, bf16[192,384]{1,0:T(8,128)(2,1)}, u32[]{:S(2)}, u32[]{:S(2)}) collective-permute-start(bf16[192,384]{1,0:T(8,128)(2,1)S(1)} %fusion.62), channel_id=1, source_target_pairs={{0,16},{1,17},{2,18},{3,19},{4,20},{5,21},{6,22},{7,23},{8,24},{9,... | collective-permute-start | bytes 442376 | tf_op jit(solution)/shard_map/ppermute | solution.py:192
  362.9 31.6 %collective-permute-start.47 = (bf16[384,768]{1,0:T(8,128)(2,1)S(1)}, bf16[384,768]{1,0:T(8,128)(2,1)S(1)}, u32[]{:S(2)}, u32[]{:S(2)}) collective-permute-start(bf16[384,768]{1,0:T(8,128)(2,1)S(1)} %bitcast.287), channel_id=1, source_target_pairs={{0,4},{1,3},{2,6},{3,1},{4,0},{5,7},{6,2},{7,5},{8,12},{9,11},{10,... | collective-permute-start | bytes 1769480 | tf_op jit(solution)/shard_map/ppermute | solution.py:192
  383.5 20.8 %collective-permute-start.38 = (bf16[768,384]{1,0:T(8,128)(2,1)S(1)}, bf16[768,384]{1,0:T(8,128)(2,1)S(1)}, u32[]{:S(2)}, u32[]{:S(2)}) collective-permute-start(bf16[768,384]{1,0:T(8,128)(2,1)S(1)} %bitcast.290), channel_id=1, source_target_pairs={{0,4},{1,3},{2,6},{3,1},{4,0},{5,7},{6,2},{7,5},{8,12},{9,11},{10,... | collective-permute-start | bytes 1769480 | tf_op jit(solution)/shard_map/ppermute | solution.py:192
  398.4 20.3 %collective-permute-start.48 = (bf16[2,384,768]{2,1,0:T(8,128)(2,1)S(1)}, bf16[2,384,768]{2,1,0:T(8,128)(2,1)S(1)}, u32[]{:S(2)}, u32[]{:S(2)}) collective-permute-start(bf16[2,384,768]{2,1,0:T(8,128)(2,1)S(1)} %pad_maximum_fusion.9), channel_id=1, source_target_pairs={{0,2},{1,5},{2,0},{3,7},{4,6},{5,1},{6,4},{7,3},{8,10},{9,13},{10,... | collective-permute-start | bytes 3538952 | tf_op jit(solution)/shard_map/ppermute | solution.py:192
  404.5 27.5 %collective-permute-start.39 = (bf16[2,768,384]{2,1,0:T(8,128)(2,1)S(1)}, bf16[2,768,384]{2,1,0:T(8,128)(2,1)S(1)}, u32[]{:S(2)}, u32[]{:S(2)}) collective-permute-start(bf16[2,768,384]{2,1,0:T(8,128)(2,1)S(1)} %pad_maximum_fusion.8), channel_id=1, source_target_pairs={{0,2},{1,5},{2,0},{3,7},{4,6},{5,1},{6,4},{7,3},{8,10},{9,13},{10,... | collective-permute-start | bytes 3538952 | tf_op jit(solution)/shard_map/ppermute | solution.py:192
  418.6 59.8 %collective-permute-start.25 = (bf16[4,192,384]{2,1,0:T(8,128)(2,1)S(1)}, bf16[4,192,384]{2,1,0:T(8,128)(2,1)S(1)}, u32[]{:S(2)}, u32[]{:S(2)}) collective-permute-start(bf16[4,192,384]{2,1,0:T(8,128)(2,1)S(1)} %pad_maximum_fusion.13.mine_ref), channel_id=1, source_target_pairs={{0,1},{1,0},{2,3},{3,2},{4,5},{5,4},{6,7},{7,6},{8,9},{9,8},{10,11... | collective-permute-start | bytes 1769480 | tf_op jit(solution)/shard_map/ppermute | solution.py:192
  419.0 119.6 %collective-permute-start.49 = (bf16[4,384,768]{2,1,0:T(8,128)(2,1)S(1)}, bf16[4,384,768]{2,1,0:T(8,128)(2,1)}, u32[]{:S(2)}, u32[]{:S(2)}) collective-permute-start(bf16[4,384,768]{2,1,0:T(8,128)(2,1)S(1)} %pad_maximum_fusion.3.mine_ref), channel_id=1, source_target_pairs={{0,1},{1,0},{2,3},{3,2},{4,5},{5,4},{6,7},{7,6},{8,9},{9,8},{10,11... | collective-permute-start | bytes 7077896 | tf_op jit(solution)/shard_map/ppermute | solution.py:192
  429.3 52.9 %collective-permute-start.11 = (bf16[2,192,1152]{2,1,0:T(8,128)(2,1)}, bf16[2,192,1152]{2,1,0:T(8,128)(2,1)}, u32[]{:S(2)}, u32[]{:S(2)}) collective-permute-start(bf16[2,192,1152]{2,1,0:T(8,128)(2,1)} %pad_maximum_fusion.10), channel_id=1, source_target_pairs={{0,2},{1,5},{2,0},{3,7},{4,6},{5,1},{6,4},{7,3},{8,10},{9,13},{10,... | collective-permute-start | bytes 2654216 | tf_op jit(solution)/shard_map/ppermute | solution.py:192
  433.7 96.3 %collective-permute-start.40 = (bf16[4,768,384]{2,1,0:T(8,128)(2,1)}, bf16[4,768,384]{2,1,0:T(8,128)(2,1)}, u32[]{:S(2)}, u32[]{:S(2)}) collective-permute-start(bf16[4,768,384]{2,1,0:T(8,128)(2,1)} %pad_maximum_fusion.2.mine_ref), channel_id=1, source_target_pairs={{0,1},{1,0},{2,3},{3,2},{4,5},{5,4},{6,7},{7,6},{8,9},{9,8},{10,11... | collective-permute-start | bytes 7077896 | tf_op jit(solution)/shard_map/ppermute | solution.py:192
  484.9 61.5 %collective-permute-start.12 = (bf16[4,192,1152]{2,1,0:T(8,128)(2,1)}, bf16[4,192,1152]{2,1,0:T(8,128)(2,1)}, u32[]{:S(2)}, u32[]{:S(2)}) collective-permute-start(bf16[4,192,1152]{2,1,0:T(8,128)(2,1)} %pad_maximum_fusion.4.mine_ref), channel_id=1, source_target_pairs={{0,1},{1,0},{2,3},{3,2},{4,5},{5,4},{6,7},{7,6},{8,9},{9,8},{10,11... | collective-permute-start | bytes 5308424 | tf_op jit(solution)/shard_map/ppermute | solution.py:192
  (90 other events, 802.3 us)
